TPU v7x, 128 devices: a whole 4x4x4 slice. The times are simulated.
128 devices in a mesh: gx: 8 (over x, core), gy: 16 (over z, y).
Axes of the slice: x: 4, y: 4, z: 4, core: 2. Of those that a mesh axis runs over, the one named last changes fastest.
Arguments:
- grad_cells: float32 [3, 32, 128, 2048], P(None, None, 'gx', 'gy'), may hold values from -6 to 6
- grad_segs: float32 [3, 131072], P(None, ('gx', 'gy')), may hold values from -6 to 6
- cell_diag: float32 [3, 3, 32, 128, 2048], P(None, None, None, 'gx', 'gy'), may hold values from -1.2 to 8, as said below
- cell_off: float32 [6, 3, 3, 32, 128, 2048], P(None, None, None, None, 'gx', 'gy'), may hold values from -1.2 to 1.2
- seg_diag: float32 [3, 3, 131072], P(None, None, ('gx', 'gy')), may hold values from -1.2 to 8, as said below
- seg_chain: float32 [2, 3, 3, 131072], P(None, None, None, ('gx', 'gy')), may hold values from -1.8 to 1.8
- seg_len: int32 [4096], P(('gx', 'gy')), may hold values from 8 to 32
- perf_device: int32 [524288, 1], P(('gx', 'gy')), may hold values from 0 to 127; in each aligned block of 4096 rows (0 to 4095, 4096 to 8191, ...) at most 64 rows name the same one
- perf_local: int32 [524288], P(('gx', 'gy')), may hold values from 0 to 65535
- perf_seg: int32 [524288], P(('gx', 'gy')), may hold values from 0 to 1023, as said below
- perf_blocks: float32 [2, 3, 3, 524288], P(None, None, None, ('gx', 'gy')), may hold values from -2.4 to 2.4
Outputs:
- adjoint_cells: float32 [3, 32, 128, 2048], P(None, None, 'gx', 'gy')
- adjoint_segs: float32 [3, 131072], P(None, ('gx', 'gy'))
- residual_cells: float32 [3, 32, 128, 2048], P(None, None, 'gx', 'gy')
- residual_segs: float32 [3, 131072], P(None, ('gx', 'gy'))
Inputs may be any that keep to these rules, and one draw needn't show every extreme that they name: `perf_device`: in the rows of one device (aligned blocks of 4096 rows) no device index appears more than 64 times. `perf_seg`: perforation r names slot w * 32 + k of device r // 4096, where w is one of that device's wells and k is below that well's seg_len. `cell_diag`: diagonal entries lie in 4 to 8, the others in -1.2 to 1.2. `seg_diag`: diagonal entries lie in 4 to 8, the others in -1.2 to 1.2.
All inputs are finite; a program needn't handle non-finite values.
Results may differ from a plain program's by a relative error of at most 0.0003.
Values sent between devices are 32-bit elements; how exact they have to be, the bound alone decides.
A program may use at most 256 MiB of HBM per device.

v0:
```python
import jax
import jax.numpy as jnp
from jax import lax
from jax.sharding import PartitionSpec as P


def with_halo(block, sides, width):
    for axis, dim in sides:
        count = lax.axis_size(axis)
        forward = [(i, i + 1) for i in range(count - 1)]
        backward = [(target, source) for source, target in forward]
        low = lax.ppermute(
            lax.slice_in_dim(block, block.shape[dim] - width, None, axis=dim), axis, forward
        )
        high = lax.ppermute(lax.slice_in_dim(block, 0, width, axis=dim), axis, backward)
        block = jnp.concatenate([low, block, high], axis=dim)
    return block


def apply_transpose(blocks, vector):
    return jnp.sum(blocks * vector[:, None], axis=0)


def inverse_transpose(matrix):
    cofactor = [
        [
            matrix[(i + 1) % 3, (j + 1) % 3] * matrix[(i + 2) % 3, (j + 2) % 3]
            - matrix[(i + 1) % 3, (j + 2) % 3] * matrix[(i + 2) % 3, (j + 1) % 3]
            for j in range(3)
        ]
        for i in range(3)
    ]
    determinant = (
        matrix[0, 0] * cofactor[0][0]
        + matrix[0, 1] * cofactor[0][1]
        + matrix[0, 2] * cofactor[0][2]
    )
    return jnp.stack([jnp.stack(row_list) for row_list in cofactor]) / determinant


def apply_inverse(inverse, vector):
    return jnp.sum(inverse * vector[None], axis=1)


def segment_couple(adjoint, seg_diag, seg_chain, well_count, seg_slots):
    result = apply_transpose(seg_diag, adjoint).reshape(3, well_count, seg_slots)
    lower = apply_transpose(seg_chain[0], adjoint).reshape(3, well_count, seg_slots)
    upper = apply_transpose(seg_chain[1], adjoint).reshape(3, well_count, seg_slots)
    result = result.at[:, :, :-1].add(lower[:, :, 1:])
    result = result.at[:, :, 1:].add(upper[:, :, :-1])
    return result.reshape(3, -1)


def shards(
    grad_cells,
    grad_segs,
    cell_diag,
    cell_off,
    seg_diag,
    seg_chain,
    seg_len,
    perf_device,
    perf_local,
    perf_seg,
    perf_blocks,
):
    grid_x = lax.axis_size("gx")
    grid_y = lax.axis_size("gy")
    count_devices = grid_x * grid_y
    width_x = grad_cells.shape[2]
    width_y = grad_cells.shape[3]
    wells_here = seg_len.shape[0]
    seg_slots = grad_segs.shape[1] // wells_here
    perfs_here = perf_local.shape[0]
    capacity = max(2, 2 * perfs_here // count_devices)
    slots_total = count_devices * capacity
    target = perf_device[:, 0]
    matches = (target[:, None] == jnp.arange(count_devices, dtype=jnp.int32)[None, :]).astype(
        jnp.int32
    )
    before = jnp.sum((jnp.cumsum(matches, axis=0) - matches) * matches, axis=1)
    slot_index = target * capacity + before
    slot_source = (
        jnp.zeros((slots_total,), jnp.int32)
        .at[slot_index]
        .set(jnp.arange(perfs_here, dtype=jnp.int32))
    )
    slot_filled = jnp.zeros((slots_total,), jnp.float32).at[slot_index].set(1.0)
    index_out = perf_local[slot_source] * slot_filled.astype(jnp.int32)
    index_in = lax.all_to_all(index_out, ("gx", "gy"), split_axis=0, concat_axis=0, tiled=True)
    active = (
        (jnp.arange(seg_slots, dtype=jnp.int32)[None, :] < seg_len[:, None])
        .reshape(-1)
        .astype(jnp.float32)
    )
    cell_inverse = inverse_transpose(cell_diag)
    seg_inverse = inverse_transpose(seg_diag)

    def horizontal(adjoint):
        moved = jnp.sum(cell_off[:4] * adjoint[None, :, None], axis=1)
        padded = with_halo(moved, (("gx", 3), ("gy", 4)), 1)
        result = (
            padded[0, :, :, 0:width_x, 1 : width_y + 1]
            + padded[1, :, :, 2 : width_x + 2, 1 : width_y + 1]
        )
        result = (
            result
            + padded[2, :, :, 1 : width_x + 1, 0:width_y]
            + padded[3, :, :, 1 : width_x + 1, 2 : width_y + 2]
        )
        return result

    def couple(cells, segs):
        cell_out = apply_transpose(cell_diag, cells) + horizontal(cells)
        rising = apply_transpose(cell_off[4], cells)
        falling = apply_transpose(cell_off[5], cells)
        cell_out = cell_out.at[:, 1:].add(rising[:, :-1])
        cell_out = cell_out.at[:, :-1].add(falling[:, 1:])
        cell_flat = cell_out.reshape(3, -1)
        cells_flat = cells.reshape(3, -1)
        pushed = apply_transpose(perf_blocks[0], segs[:, perf_seg])
        send_push = pushed[:, slot_source] * slot_filled[None, :]
        send_pull = cells_flat[:, index_in]
        got_push, got_pull = (
            lax.all_to_all(send_push, ("gx", "gy"), split_axis=1, concat_axis=1, tiled=True),
            lax.all_to_all(send_pull, ("gx", "gy"), split_axis=1, concat_axis=1, tiled=True),
        )
        cell_flat = cell_flat.at[:, index_in].add(got_push)
        seg_out = segment_couple(segs, seg_diag, seg_chain, wells_here, seg_slots)
        seg_out = seg_out.at[:, perf_seg].add(
            apply_transpose(perf_blocks[1], got_pull[:, slot_index])
        )
        return (cell_flat.reshape(cells.shape), seg_out)

    adjoint_cells = apply_inverse(cell_inverse, grad_cells)
    adjoint_segs = active * apply_inverse(seg_inverse, grad_segs)
    image_cells, image_segs = couple(adjoint_cells, adjoint_segs)
    adjoint_cells = adjoint_cells + apply_inverse(cell_inverse, grad_cells - image_cells)
    adjoint_segs = adjoint_segs + active * apply_inverse(seg_inverse, grad_segs - image_segs)
    image_cells, image_segs = couple(adjoint_cells, adjoint_segs)
    residual_cells = grad_cells - image_cells
    residual_segs = active * (grad_segs - image_segs)
    return (adjoint_cells, adjoint_segs, residual_cells, residual_segs)


def solution(mesh):
    in_specs = (
        P(None, None, "gx", "gy"),
        P(None, ("gx", "gy")),
        P(None, None, None, "gx", "gy"),
        P(None, None, None, None, "gx", "gy"),
        P(None, None, ("gx", "gy")),
        P(None, None, None, ("gx", "gy")),
        P(("gx", "gy")),
        P(("gx", "gy"), None),
        P(("gx", "gy")),
        P(("gx", "gy")),
        P(None, None, None, ("gx", "gy")),
    )
    out_specs = (
        P(None, None, "gx", "gy"),
        P(None, ("gx", "gy")),
        P(None, None, "gx", "gy"),
        P(None, ("gx", "gy")),
    )
    return jax.shard_map(shards, mesh=mesh, in_specs=in_specs, out_specs=out_specs, check_vma=False)
```

profile of v0, /device:TPU:1, one launch (start us, length us, event | category | flops | bytes accessed | tf_op | source)
XLA Modules:
  0.0 930.9 jit_solution(7680370290170221901)
XLA Ops:
  22.3 15.5 %scatter_custom_fusion = s32[8192]{0:T(1024)S(1)} fusion(s32[4096]{0:T(1024)S(1)} %bitcast.215, s32[4096]{0:T(1024)S(1)} %iota.15, s32[]{:T(128)} %constant.200.clone.1), kind=kCustom, calls=%fused_computation.133 | custom fusion | bytes 32772 | tf_op jit(solution)/shard_map/scatter | solution.py:86
  37.9 45.5 %gather_fusion = s32[8192]{0:T(1024)S(1)} fusion(s32[4096]{0:T(1024)S(1)} %copy-done, s32[8192]{0:T(1024)S(1)} %fusion.33), kind=kCustom, calls=%fused_computation | custom fusion | bytes 98304 | tf_op jit(solution)/shard_map/gather | solution.py:89
  83.5 15.5 %scatter_custom_fusion.1 = f32[8192]{0:T(1024)S(1)} fusion(s32[4096]{0:T(1024)S(1)} %bitcast.216, f32[4096]{0:T(1024)S(1)} %broadcast.227, f32[]{:T(128)} %constant.199.clone.1), kind=kCustom, calls=%fused_computation.131 | custom fusion | bytes 32772 | tf_op jit(solution)/shard_map/scatter | solution.py:88
  127.5 15.1 %gather_fusion.1 = f32[4096,3]{1,0:T(8,128)} fusion(f32[3,1024]{0,1:T(8,128)} %copy.264, s32[4096]{0:T(1024)S(1)} %get-tuple-element.177), kind=kCustom, calls=%fused_computation.1 | custom fusion | bytes 114688 | tf_op jit(solution)/shard_map/gather | solution.py:121
  150.0 32.0 %gather_fusion.2 = f32[8192,3]{1,0:T(8,128)} fusion(f32[3,4096]{0,1:T(8,128)} %copy.266, s32[8192]{0:T(1024)} %copy-done.21), kind=kCustom, calls=%fused_computation.2 | custom fusion | bytes 229376 | tf_op jit(solution)/shard_map/gather | solution.py:122
  203.0 16.5 %copy.276 = f32[3,32,16,128]{0,3,2,1:T(8,128)} copy(f32[3,32,16,128]{3,2,1,0:T(8,128)S(1)} %multiply_reduce_fusion.5) | data formatting | bytes 1572864 | tf_op jit(solution)/shard_map/reduce_sum | solution.py:42
  237.9 40.9 %gather_fusion.3 = f32[8192,3]{1,0:T(8,128)} fusion(f32[3,65536]{0,1:T(8,128)} %bitcast.171, s32[8192]{0:T(1024)} %broadcast_clamp_fusion), kind=kCustom, calls=%fused_computation.3 | custom fusion | bytes 229376 | tf_op jit(solution)/shard_map/gather | solution.py:123
  307.0 12.4 %all-to-all-start.2 = ((f32[128,1,192]{2,1,0:T(1,128)}), f32[128,1,192]{2,1,0:T(1,128)}, u32[]{:S(2)}, u32[]{:S(2)}) async-start(f32[128,1,192]{2,1,0:T(1,128)} %reshape.1331), calls=%async_computation.2 | async-start | bytes 262144 | tf_op jit(solution)/shard_map/all_to_all | solution.py:126
  343.7 17.6 %gather_fusion.4 = f32[4096,3]{1,0:T(8,128)} fusion(f32[3,8192]{0,1:T(8,128)} %bitcast.183, s32[4096]{0:T(1024)} %broadcast_clamp_fusion.1), kind=kCustom, calls=%fused_computation.4 | custom fusion | bytes 114688 | tf_op jit(solution)/shard_map/gather | solution.py:131
  381.7 17.1 %copy.260 = f32[3,32,16,128]{0,3,2,1:T(8,128)} copy(f32[3,32,16,128]{3,2,1,0:T(8,128)} %fusion.21) | data formatting | bytes 1572864 | tf_op jit(solution)/shard_map/scatter-add | solution.py:118
  398.8 71.1 %scatter_fusion = f32[3,65536]{0,1:T(8,128)} fusion(f32[3,65536]{0,1:T(8,128)} %bitcast.174, s32[8192]{0:T(1024)} %bitcast.206, f32[8192,3]{1,0:T(8,128)} %copy.269), kind=kCustom, calls=%fused_computation.11 | custom fusion | flops 24576 | bytes 327680 | tf_op jit(solution)/shard_map/scatter-add | solution.py:128
  469.9 19.5 %copy.270 = f32[3,32,16,128]{3,2,1,0:T(8,128)} copy(f32[3,32,16,128]{0,3,2,1:T(8,128)} %bitcast.175) | data formatting | bytes 1572864 | tf_op jit(solution)/shard_map/reshape | solution.py:133
  494.8 17.2 %copy.304 = f32[3,32,16,128]{0,3,2,1:T(8,128)} copy(f32[3,32,16,128]{3,2,1,0:T(8,128)} %copy-done.12) | data formatting | bytes 1572864 | tf_op jit(solution)/shard_map/reduce_sum | solution.py:42
  522.1 33.3 %bitcast_add_fusion = f32[3,65536]{0,1:T(8,128)} fusion(f32[3,32,16,128]{0,3,2,1:T(8,128)} %copy.304, f32[3,32,16,128]{0,3,2,1:T(8,128)} %copy.276), kind=kLoop, calls=%fused_computation.15 | loop fusion | flops 196608 | bytes 2359296 | tf_op jit(solution)/shard_map/add | solution.py:138
  555.4 38.2 %gather_fusion.7 = f32[8192,3]{1,0:T(8,128)} fusion(f32[3,65536]{0,1:T(8,128)} %bitcast_add_fusion, s32[8192]{0:T(1024)S(1)} %copy-done.27), kind=kCustom, calls=%fused_computation.7 | custom fusion | bytes 229376 | tf_op jit(solution)/shard_map/gather | solution.py:123
  597.6 10.9 %all-to-all-start.4 = ((f32[128,1,192]{2,1,0:T(1,128)}), f32[128,1,192]{2,1,0:T(1,128)S(1)}, u32[]{:S(2)}, u32[]{:S(2)}) async-start(f32[128,1,192]{2,1,0:T(1,128)} %reshape.1329), calls=%async_computation.4 | async-start | bytes 262144 | tf_op jit(solution)/shard_map/all_to_all | solution.py:126
  624.1 17.6 %gather_fusion.8 = f32[4096,3]{1,0:T(8,128)} fusion(f32[3,8192]{0,1:T(8,128)} %bitcast.182, s32[4096]{0:T(1024)} %broadcast_clamp_fusion.1), kind=kCustom, calls=%fused_computation.8 | custom fusion | bytes 114688 | tf_op jit(solution)/shard_map/gather | solution.py:131
  647.7 22.4 %scatter_fusion.1 = f32[3,1024]{0,1:T(8,128)} fusion(f32[3,1024]{0,1:T(8,128)} %bitcast.178, s32[4096]{0:T(1024)S(1)} %get-tuple-element.176, f32[4096,3]{1,0:T(8,128)} %copy.280), kind=kCustom, calls=%fused_computation.12 | custom fusion | flops 12288 | bytes 163840 | tf_op jit(solution)/shard_map/scatter-add | solution.py:130
  678.0 15.1 %gather_fusion.5 = f32[4096,3]{1,0:T(8,128)} fusion(f32[3,1024]{0,1:T(8,128)} %copy.293, s32[4096]{0:T(1024)S(1)} %get-tuple-element.177), kind=kCustom, calls=%fused_computation.5 | custom fusion | bytes 114688 | tf_op jit(solution)/shard_map/gather | solution.py:121
  697.4 29.3 %gather_fusion.6 = f32[8192,3]{1,0:T(8,128)} fusion(f32[3,4096]{0,1:T(8,128)} %copy.295, s32[8192]{0:T(1024)S(1)} %copy-done.22), kind=kCustom, calls=%fused_computation.6 | custom fusion | bytes 229376 | tf_op jit(solution)/shard_map/gather | solution.py:122
  754.2 22.2 %scatter_fusion.3 = f32[3,1024]{0,1:T(8,128)} fusion(f32[3,1024]{0,1:T(8,128)} %bitcast.181, s32[4096]{0:T(1024)S(1)} %get-tuple-element.176, f32[4096,3]{1,0:T(8,128)} %copy.308), kind=kCustom, calls=%fused_computation.14 | custom fusion | flops 12288 | bytes 163840 | tf_op jit(solution)/shard_map/scatter-add | solution.py:130
  822.7 17.4 %copy.292 = f32[3,32,16,128]{0,3,2,1:T(8,128)} copy(f32[3,32,16,128]{3,2,1,0:T(8,128)} %fusion.19) | data formatting | bytes 1572864 | tf_op jit(solution)/shard_map/scatter-add | solution.py:118
  840.1 70.7 %scatter_fusion.2 = f32[3,65536]{0,1:T(8,128)} fusion(f32[3,65536]{0,1:T(8,128)} %bitcast.172, s32[8192]{0:T(1024)S(1)} %bitcast.207, f32[8192,3]{1,0:T(8,128)} %copy.298), kind=kCustom, calls=%fused_computation.13 | custom fusion | flops 24576 | bytes 327680 | tf_op jit(solution)/shard_map/scatter-add | solution.py:128
  910.8 18.8 %copy.299 = f32[3,32,16,128]{3,2,1,0:T(8,128)S(1)} copy(f32[3,32,16,128]{0,3,2,1:T(8,128)} %bitcast.173) | data formatting | bytes 1572864 | tf_op jit(solution)/shard_map/reshape | solution.py:133
  (233 shorter events, 297.3 us)
Async XLA Ops:
  0.6 37.3 %copy-start = (s32[4096]{0:T(1024)S(1)}, s32[4096]{0:T(1024)}, u32[]{:S(2)}) copy-start(s32[4096]{0:T(1024)} %param.35) | copy-start | bytes 49156
  12.1 272.1 %collective-permute-start.1 = (f32[4,3,32,1,128]{4,2,3,1,0:T(8,128)}, f32[4,3,32,1,128]{4,2,3,1,0:T(8,128)}, u32[]{:S(2)}, u32[]{:S(2)}) collective-permute-start(f32[4,3,32,1,128]{4,2,3,1,0:T(8,128)} %bitcast.15), channel_id=1, source_target_pairs={{16,0},{32,16},{48,32},{64,48},{80,64},{96,80},{112,96},{17,1},{33... | collective-permute-start | bytes 589832 | tf_op jit(solution)/shard_map/ppermute | solution.py:15
  15.4 268.8 %collective-permute-start = (f32[4,3,32,1,128]{4,2,3,1,0:T(8,128)}, f32[4,3,32,1,128]{4,2,3,1,0:T(8,128)}, u32[]{:S(2)}, u32[]{:S(2)}) collective-permute-start(f32[4,3,32,1,128]{4,2,3,1,0:T(8,128)} %bitcast.13), channel_id=1, source_target_pairs={{0,16},{16,32},{32,48},{48,64},{64,80},{80,96},{96,112},{1,17},{17... | collective-permute-start | bytes 589832 | tf_op jit(solution)/shard_map/ppermute | solution.py:12
  22.3 61.2 %copy-start.38 = (s32[4096,1]{0,1:T(1,128)}, s32[4096,1]{0,1:T(1,128)S(1)}, u32[]{:S(2)}) copy-start(s32[4096,1]{0,1:T(1,128)S(1)} %compare_select_fusion.1) | copy-start | bytes 49156
  37.9 45.6 %copy-start.21 = (s32[8192]{0:T(1024)}, s32[8192]{0:T(1024)S(1)}, u32[]{:S(2)}) copy-start(s32[8192]{0:T(1024)S(1)} %fusion.33) | copy-start | bytes 98308
  37.9 72.8 %copy-start.3 = (f32[3,3,32,16,128]{4,3,2,1,0:T(8,128)S(1)}, f32[3,3,32,16,128]{4,3,2,1,0:T(8,128)}, u32[]{:S(2)}) copy-start(f32[3,3,32,16,128]{4,3,2,1,0:T(8,128)} %param.29) | copy-start | bytes 7077892
  99.8 121.5 %all-to-all-start = ((s32[128,64,1]{1,2,0:T(1,128)}), s32[128,64,1]{1,2,0:T(1,128)}, u32[]{:S(2)}, u32[]{:S(2)}) async-start(s32[128,64,1]{1,2,0:T(1,128)} %bitcast.28), calls=%async_computation | async-start | bytes 131072 | tf_op jit(solution)/shard_map/all_to_all | solution.py:90
  221.3 85.6 %all-to-all-start.1 = ((f32[128,1,192]{2,1,0:T(1,128)}), f32[128,1,192]{2,1,0:T(1,128)}, u32[]{:S(2)}, u32[]{:S(2)}) async-start(f32[128,1,192]{2,1,0:T(1,128)} %reshape.1327), calls=%async_computation.1 | async-start | bytes 262144 | tf_op jit(solution)/shard_map/all_to_all | solution.py:125
  296.6 67.5 %collective-permute-start.3 = (f32[4,3,32,18,1]{2,0,4,3,1:T(4,128)}, f32[4,3,32,18,1]{2,0,4,3,1:T(4,128)}, u32[]{:S(2)}, u32[]{:S(2)}) collective-permute-start(f32[4,3,32,18,1]{2,0,4,3,1:T(4,128)} %copy.258), channel_id=1, source_target_pairs={{1,0},{2,1},{3,2},{4,3},{5,4},{6,5},{7,6},{8,7},{9,8},{10,9},{11,1... | collective-permute-start | bytes 82952 | tf_op jit(solution)/shard_map/ppermute | solution.py:15
  302.3 66.2 %collective-permute-start.2 = (f32[4,3,32,18,1]{2,0,4,3,1:T(4,128)}, f32[4,3,32,18,1]{2,0,4,3,1:T(4,128)}, u32[]{:S(2)}, u32[]{:S(2)}) collective-permute-start(f32[4,3,32,18,1]{2,0,4,3,1:T(4,128)} %copy.256), channel_id=1, source_target_pairs={{0,1},{1,2},{2,3},{3,4},{4,5},{5,6},{6,7},{7,8},{8,9},{9,10},{10,1... | collective-permute-start | bytes 82952 | tf_op jit(solution)/shard_map/ppermute | solution.py:12
  307.0 28.8 %all-to-all-start.2 = ((f32[128,1,192]{2,1,0:T(1,128)}), f32[128,1,192]{2,1,0:T(1,128)}, u32[]{:S(2)}, u32[]{:S(2)}) async-start(f32[128,1,192]{2,1,0:T(1,128)} %reshape.1331), calls=%async_computation.2 | async-start | bytes 262144 | tf_op jit(solution)/shard_map/all_to_all | solution.py:126
  522.1 33.4 %copy-start.27 = (s32[8192]{0:T(1024)S(1)}, s32[8192]{0:T(1024)}, u32[]{:S(2)}) copy-start(s32[8192]{0:T(1024)} %broadcast_clamp_fusion) | copy-start | bytes 98308
  597.6 21.1 %all-to-all-start.4 = ((f32[128,1,192]{2,1,0:T(1,128)}), f32[128,1,192]{2,1,0:T(1,128)S(1)}, u32[]{:S(2)}, u32[]{:S(2)}) async-start(f32[128,1,192]{2,1,0:T(1,128)} %reshape.1329), calls=%async_computation.4 | async-start | bytes 262144 | tf_op jit(solution)/shard_map/all_to_all | solution.py:126
  609.7 168.0 %collective-permute-start.5 = (f32[4,3,32,1,128]{4,2,3,1,0:T(8,128)}, f32[4,3,32,1,128]{4,2,3,1,0:T(8,128)}, u32[]{:S(2)}, u32[]{:S(2)}) collective-permute-start(f32[4,3,32,1,128]{4,2,3,1,0:T(8,128)} %bitcast.61), channel_id=1, source_target_pairs={{16,0},{32,16},{48,32},{64,48},{80,64},{96,80},{112,96},{17,1},{33... | collective-permute-start | bytes 589832 | tf_op jit(solution)/shard_map/ppermute | solution.py:15
  612.6 165.1 %collective-permute-start.4 = (f32[4,3,32,1,128]{4,2,3,1,0:T(8,128)}, f32[4,3,32,1,128]{4,2,3,1,0:T(8,128)}, u32[]{:S(2)}, u32[]{:S(2)}) collective-permute-start(f32[4,3,32,1,128]{4,2,3,1,0:T(8,128)} %bitcast.59), channel_id=1, source_target_pairs={{0,16},{16,32},{32,48},{48,64},{64,80},{80,96},{96,112},{1,17},{17... | collective-permute-start | bytes 589832 | tf_op jit(solution)/shard_map/ppermute | solution.py:12
  641.7 31.8 %copy-start.39 = (f32[1024]{0:T(1024)S(1)}, f32[1024]{0:T(1024)}, u32[]{:S(2)}) copy-start(f32[1024]{0:T(1024)} %reshape.1186) | copy-start | bytes 12292
  641.7 34.9 %copy-start.24 = (f32[1,3,3,1024]{3,0,2,1:T(1,128)S(1)}, f32[1,3,3,1024]{3,0,2,1:T(1,128)}, u32[]{:S(2)}) copy-start(f32[1,3,3,1024]{3,0,2,1:T(1,128)} %copy-done.23) | copy-start | bytes 110596
  641.7 34.9 %copy-start.26 = (f32[1,3,3,1024]{3,0,2,1:T(1,128)S(1)}, f32[1,3,3,1024]{3,0,2,1:T(1,128)}, u32[]{:S(2)}) copy-start(f32[1,3,3,1024]{3,0,2,1:T(1,128)} %copy-done.25) | copy-start | bytes 110596
  647.7 47.6 %copy-start.17 = (f32[1,3,3,4096]{3,0,2,1:T(1,128)S(1)}, f32[1,3,3,4096]{3,0,2,1:T(1,128)}, u32[]{:S(2)}) copy-start(f32[1,3,3,4096]{3,0,2,1:T(1,128)} %get-tuple-element.163) | copy-start | bytes 442372
  671.9 25.5 %copy-start.22 = (s32[8192]{0:T(1024)S(1)}, s32[8192]{0:T(1024)}, u32[]{:S(2)}) copy-start(s32[8192]{0:T(1024)} %copy-done.21) | copy-start | bytes 98308
  732.3 68.1 %all-to-all-start.3 = ((f32[128,1,192]{2,1,0:T(1,128)}), f32[128,1,192]{2,1,0:T(1,128)S(1)}, u32[]{:S(2)}, u32[]{:S(2)}) async-start(f32[128,1,192]{2,1,0:T(1,128)} %reshape.1333), calls=%async_computation.3 | async-start | bytes 262144 | tf_op jit(solution)/shard_map/all_to_all | solution.py:125
  789.1 16.9 %collective-permute-start.7 = (f32[4,3,32,18,1]{2,0,4,3,1:T(4,128)}, f32[4,3,32,18,1]{2,0,4,3,1:T(4,128)}, u32[]{:S(2)}, u32[]{:S(2)}) collective-permute-start(f32[4,3,32,18,1]{2,0,4,3,1:T(4,128)} %copy.290), channel_id=1, source_target_pairs={{1,0},{2,1},{3,2},{4,3},{5,4},{6,5},{7,6},{8,7},{9,8},{10,9},{11,1... | collective-permute-start | bytes 82952 | tf_op jit(solution)/shard_map/ppermute | solution.py:15
  795.0 15.3 %collective-permute-start.6 = (f32[4,3,32,18,1]{2,0,4,3,1:T(4,128)}, f32[4,3,32,18,1]{2,0,4,3,1:T(4,128)}, u32[]{:S(2)}, u32[]{:S(2)}) collective-permute-start(f32[4,3,32,18,1]{2,0,4,3,1:T(4,128)} %copy.288), channel_id=1, source_target_pairs={{0,1},{1,2},{2,3},{3,4},{4,5},{5,6},{6,7},{7,8},{8,9},{9,10},{10,1... | collective-permute-start | bytes 82952 | tf_op jit(solution)/shard_map/ppermute | solution.py:12
  910.8 19.8 %copy-start.1 = (s32[4096]{0:T(1024)S(1)}, s32[4096]{0:T(1024)}, u32[]{:S(2)}) copy-start(s32[4096]{0:T(1024)} %param.35) | copy-start | bytes 49156
  (30 other events, 205.7 us)
where the time goes:
time: 946 us; the launch traced here: 931 us
  local copies, waits for them, and re-layouts  542 us (57%)
  other arithmetic  310 us (33%)
  starting transfers between devices  74.6 us (8%)
    scatter-add x2, other arithmetic, couple(): cell_flat = cell_flat.at[:, index_in].add(got_push)  142 us
    gather x2, local copies, waits for them, and re-layouts, couple(): send_pull = cells_flat[:, index_in]  79.2 us
    gather x4, local copies, waits for them, and re-layouts, couple(): send_push = pushed[:, slot_source] * slot_filled[None, :]  67.9 us
    gather x1, local copies, waits for them, and re-layouts, shards(): index_out = perf_local[slot_source] * slot_filled.astype(jnp.int32)  45.5 us
    scatter-add x2, other arithmetic, couple(): seg_out.at[:, perf_seg]  44.6 us
    gather x4, local copies, waits for them, and re-layouts, couple(): got_pull[:, slot_index]  40.2 us
    reshape x2, local copies, waits for them, and re-layouts, couple(): return (cell_flat.reshape(cells.shape), seg_out)  38.4 us
    gather x4, local copies, waits for them, and re-layouts, couple(): pushed = apply_transpose(perf_blocks[0], segs[:, perf_seg])  35.3 us
  transfers between devices with their start and end apart: 13, of which 1 were waited for; matrix products, arithmetic and copies ran while one was open for 52% of the time, Pallas kernels for 0%

commit v1 on v0

v1 whole, which is shorter than its diff:
```python
import jax
import jax.numpy as jnp
from jax import lax
from jax.experimental import pallas as pl
from jax.experimental.pallas import tpu as pltpu
from jax.sharding import PartitionSpec as P

MESH = pl.DeviceIdType.MESH
F32 = jnp.float32
BF16 = jnp.bfloat16
NT = (((1,), (1,)), ((), ()))
GX = 8
GY = 16
ND = GX * GY
NZ = 32
CX = 16
CY = 128
ROWS = NZ * CX
SEGS = 1024
SEG_MAX = 32
PERFS = 4096
KLO = 32
KHI = 2
WIDE = KHI * ND
SLOTS = KLO * WIDE
BUCKETS = 4
BROWS = ROWS // BUCKETS
CHUNK = 512
CHUNKS = SLOTS // CHUNK + BUCKETS
CROWS = 24
VMEM = pl.BlockSpec(memory_space=pltpu.VMEM)
ANY = pl.BlockSpec(memory_space=pl.ANY)


def rounded(x):
    return x.astype(BF16).astype(F32)


def halves(x):
    high = rounded(x)
    return high, x - high


def iota(shape, dim):
    return lax.broadcasted_iota(jnp.int32, shape, dim)


def one_hot(count, row, kind):
    hit = iota((count, row.shape[1]), 0) == row
    return hit.astype(F32).astype(kind)


def inverse_rows(matrix):
    cofactor = [
        [
            matrix[(i + 1) % 3][(j + 1) % 3] * matrix[(i + 2) % 3][(j + 2) % 3]
            - matrix[(i + 1) % 3][(j + 2) % 3] * matrix[(i + 2) % 3][(j + 1) % 3]
            for j in range(3)
        ]
        for i in range(3)
    ]
    determinant = (
        matrix[0][0] * cofactor[0][0]
        + matrix[0][1] * cofactor[0][1]
        + matrix[0][2] * cofactor[0][2]
    )
    return cofactor, 1.0 / determinant


def solve_rows(matrix, vector):
    cofactor, scale = inverse_rows(matrix)
    return [
        (cofactor[i][0] * vector[0] + cofactor[i][1] * vector[1] + cofactor[i][2] * vector[2])
        * scale
        for i in range(3)
    ]


def transposed_rows(matrix, vector):
    return [
        matrix[0][i] * vector[0] + matrix[1][i] * vector[1] + matrix[2][i] * vector[2]
        for i in range(3)
    ]


def seg_rows(ref):
    return [ref[j : j + 1, :] for j in range(3)]


def seg_matrix(ref):
    return [[ref[i, j : j + 1, :] for j in range(3)] for i in range(3)]


def active_row(seg_len_ref):
    lanes = iota((32, SEGS), 1)
    mine = (lanes // SEG_MAX) == iota((32, SEGS), 0)
    below = (lanes % SEG_MAX) < seg_len_ref[...]
    return jnp.sum(jnp.where(mine & below, 1.0, 0.0), axis=0, keepdims=True)


def seg_gather(values, seg_slots, lane_hot_ref, table_ref, out_ref):
    for c in range(3):
        high, low = halves(values[c])
        for h in range(8):
            table_ref[c * 8 + h : c * 8 + h + 1, 0:128] = high[:, 128 * h : 128 * (h + 1)]
            table_ref[c * 8 + h : c * 8 + h + 1, 128:256] = low[:, 128 * h : 128 * (h + 1)]
    table = table_ref[...].astype(BF16)

    def body(k, _):
        lanes = pl.ds(pl.multiple_of(k * WIDE, WIDE), WIDE)
        hot = lane_hot_ref[:, lanes]
        found = jnp.dot(table[:, :128], hot, preferred_element_type=F32) + jnp.dot(
            table[:, 128:], hot, preferred_element_type=F32
        )
        high = seg_slots[pl.ds(k, 1), :].astype(jnp.int32) >> 7
        pick = (iota((8, WIDE), 0) == high).astype(F32)
        for c in range(3):
            out_ref[pl.ds(c * KLO + k, 1), :] = jnp.sum(
                found[8 * c : 8 * c + 8] * pick, axis=0, keepdims=True
            )
        return 0

    lax.fori_loop(0, KLO, body, 0, unroll=4)


def seg_scatter(values_ref, seg_slots, lane_hot_ref, table_ref):
    def body(k, total):
        lanes = pl.ds(pl.multiple_of(k * WIDE, WIDE), WIDE)
        hot = lane_hot_ref[:, lanes]
        high = seg_slots[pl.ds(k, 1), :].astype(jnp.int32) >> 7
        pick = (iota((8, WIDE), 0) == high).astype(F32)
        left = []
        for c in range(3):
            left += [pick * part for part in halves(values_ref[pl.ds(c * KLO + k, 1), :])]
        return total + lax.dot_general(
            jnp.concatenate(left, axis=0).astype(BF16), hot, NT, preferred_element_type=F32
        )

    total = lax.fori_loop(0, KLO, body, jnp.zeros((48, 128), F32), unroll=4)
    rows = []
    for c in range(3):
        table_ref[0:8, 0:128] = total[16 * c : 16 * c + 8] + total[16 * c + 8 : 16 * c + 16]
        rows.append(
            jnp.concatenate([table_ref[h : h + 1, 0:128] for h in range(8)], axis=1)
        )
    return rows


def lane_hots(seg_slots, lane_hot_ref):
    def body(k, _):
        lanes = pl.ds(pl.multiple_of(k * WIDE, WIDE), WIDE)
        low = seg_slots[pl.ds(k, 1), :].astype(jnp.int32) & 127
        lane_hot_ref[:, lanes] = one_hot(128, low, BF16)
        return 0

    lax.fori_loop(0, KLO, body, 0, unroll=4)


def slot_terms(blocks, number, rows_ref, start):
    vector = [rows_ref[start + c * KLO : start + (c + 1) * KLO, :] for c in range(3)]
    out = []
    for i in range(3):
        total = None
        for j in range(3):
            at = (number * 9 + j * 3 + i) * KLO
            term = blocks[at : at + KLO, :] * vector[j]
            total = term if total is None else total + term
        out.append(total)
    return out


def everyone(act):
    gx = lax.axis_index("gx")
    gy = lax.axis_index("gy")
    me = gx * GY + gy

    def body(i, _):
        other = lax.rem(me + i, ND)
        act(other, (other // GY, lax.rem(other, GY)))
        return 0

    lax.fori_loop(1, ND, body, 0)


def greet():
    barrier = pltpu.get_barrier_semaphore()
    everyone(
        lambda other, place: pl.semaphore_signal(
            barrier, inc=1, device_id=place, device_id_type=MESH
        )
    )


def greeted():
    pl.semaphore_wait(pltpu.get_barrier_semaphore(), ND - 1)


class Exchange:
    def __init__(self, source, target, send_sem, recv_sem, own_sem):
        self.source, self.target = source, target
        self.send_sem, self.recv_sem, self.own_sem = send_sem, recv_sem, own_sem
        self.me = lax.axis_index("gx") * GY + lax.axis_index("gy")

    def own(self):
        return pltpu.make_async_copy(
            self.source.at[self.me], self.target.at[self.me], self.own_sem
        )

    def whole(self):
        return pltpu.make_async_remote_copy(
            src_ref=self.source.at[pl.ds(0, ND - 1)],
            dst_ref=self.target.at[pl.ds(0, ND - 1)],
            send_sem=self.send_sem,
            recv_sem=self.recv_sem,
            device_id=(lax.axis_index("gx"), lax.axis_index("gy")),
            device_id_type=MESH,
        )

    def start(self):
        self.own().start()
        everyone(
            lambda other, place: pltpu.make_async_remote_copy(
                src_ref=self.source.at[other],
                dst_ref=self.target.at[self.me],
                send_sem=self.send_sem,
                recv_sem=self.recv_sem,
                device_id=place,
                device_id_type=MESH,
            ).start()
        )

    def wait_recv(self):
        self.own().wait()
        self.whole().wait_recv()

    def wait_send(self):
        self.whole().wait_send()


class Halo:
    def __init__(self, x_out, x_in, y_out, y_in, send_sem, recv_sem):
        gx = lax.axis_index("gx")
        gy = lax.axis_index("gy")
        places = [
            (lax.rem(gx + 1, GX), gy),
            (lax.rem(gx + GX - 1, GX), gy),
            (gx, lax.rem(gy + 1, GY)),
            (gx, lax.rem(gy + GY - 1, GY)),
        ]
        pairs = [(x_out, x_in, 0), (x_out, x_in, 1), (y_out, y_in, 0), (y_out, y_in, 1)]
        self.copies = [
            pltpu.make_async_remote_copy(
                src_ref=a.at[n],
                dst_ref=b.at[n],
                send_sem=send_sem.at[at],
                recv_sem=recv_sem.at[at],
                device_id=place,
                device_id_type=MESH,
            )
            for at, ((a, b, n), place) in enumerate(zip(pairs, places))
        ]
        self.x_out, self.x_in, self.y_out, self.y_in = x_out, x_in, y_out, y_in

    def start(self):
        for copy in self.copies:
            copy.start()

    def wait_recv(self):
        for copy in self.copies:
            copy.wait_recv()

    def wait_send(self):
        for copy in self.copies:
            copy.wait_send()


def stencil(adjoint, diag_ref, off_ref, image_ref, halo, column_ref):
    for c in range(3):
        image_ref[c] = jnp.zeros((NZ + 2, CX, CY), F32)
    rows = iota((CX, CY), 0)
    lanes = iota((CX, CY), 1)

    def body(z, _):
        a = adjoint(z)
        own = transposed_rows([[diag_ref[j, i, z] for i in range(3)] for j in range(3)], a)
        moved = [
            transposed_rows([[off_ref[e, j, i, z] for i in range(3)] for j in range(3)], a)
            for e in range(6)
        ]
        columns = jnp.zeros((CX, CY), F32)
        for c in range(3):
            total = own[c]
            halo.x_out[0, c, pl.ds(z, 1), :] = moved[0][c][CX - 1 : CX]
            halo.x_out[1, c, pl.ds(z, 1), :] = moved[1][c][0:1]
            total += jnp.where(rows == 0, 0.0, pltpu.roll(moved[0][c], 1, 0))
            total += jnp.where(rows == CX - 1, 0.0, pltpu.roll(moved[1][c], CX - 1, 0))
            total += jnp.where(lanes == 0, 0.0, pltpu.roll(moved[2][c], 1, 1))
            total += jnp.where(lanes == CY - 1, 0.0, pltpu.roll(moved[3][c], CY - 1, 1))
            columns = jnp.where(lanes == c, pltpu.roll(moved[2][c], 1 + c, 1), columns)
            columns = jnp.where(lanes == 8 + c, pltpu.roll(moved[3][c], 8 + c, 1), columns)
            image_ref[c, z + 1] += total
            image_ref[c, z + 2] += moved[4][c]
            image_ref[c, z] += moved[5][c]
        column_ref[pl.ds(pl.multiple_of(z * CX, CX), CX), :] = columns
        return 0

    lax.fori_loop(0, NZ, body, 0, unroll=2)
    turned = column_ref[...].T
    halo.y_out[0] = turned[0:8]
    halo.y_out[1] = turned[8:16]
    halo.start()


def add_rims(image_ref, halo, column_ref):
    gx = lax.axis_index("gx")
    gy = lax.axis_index("gy")
    first_x = jnp.where(gx > 0, 1.0, 0.0)
    last_x = jnp.where(gx < GX - 1, 1.0, 0.0)
    first_y = jnp.where(gy > 0, 1.0, 0.0)
    last_y = jnp.where(gy < GY - 1, 1.0, 0.0)
    came = jnp.concatenate(
        [halo.y_in[0] * first_y, halo.y_in[1] * last_y, jnp.zeros((CY - 16, ROWS), F32)], axis=0
    )
    column_ref[...] = came.T
    rows = iota((CX, CY), 0)
    lanes = iota((CX, CY), 1)

    def body(z, _):
        columns = column_ref[pl.ds(pl.multiple_of(z * CX, CX), CX), :]
        for c in range(3):
            low = halo.x_in[0, c, pl.ds(z, 1), :] * first_x
            high = halo.x_in[1, c, pl.ds(z, 1), :] * last_x
            total = jnp.where(rows == 0, low, 0.0) + jnp.where(rows == CX - 1, high, 0.0)
            left = columns if c == 0 else pltpu.roll(columns, CY - c, 1)
            total += jnp.where(lanes == 0, left, 0.0)
            right = pltpu.roll(columns, CY - 1 - 8 - c, 1)
            total += jnp.where(lanes == CY - 1, right, 0.0)
            image_ref[c, z + 1] += total
        return 0

    lax.fori_loop(0, NZ, body, 0, unroll=2)


def rank_and_place(device_ref, x_ref, work_ref, total_ref):
    above = (iota((256, 256), 0) < iota((256, 256), 1)).astype(F32).astype(BF16)
    ones = jnp.ones((256, 256), BF16)
    carry = jnp.zeros((ND, 256), F32)
    for j in range(PERFS // 512):
        ranks = []
        for half in range(2):
            target = device_ref[:, 512 * j + 256 * half : 512 * j + 256 * (half + 1)]
            hit = one_hot(ND, target, F32)
            hit16 = hit.astype(BF16)
            before = jnp.dot(hit16, above, preferred_element_type=F32) + carry
            carry = carry + jnp.dot(hit16, ones, preferred_element_type=F32)
            ranks.append(jnp.sum(before * hit, axis=0, keepdims=True))
        rank = jnp.concatenate(ranks, axis=1).astype(jnp.int32)
        target = device_ref[:, 512 * j : 512 * (j + 1)]
        column_hot = one_hot(WIDE, target + ND * (rank >> 5), BF16)
        row_hot = one_hot(KLO, rank & (KLO - 1), F32)
        x = x_ref[:, 512 * j : 512 * (j + 1)]
        high, low = halves(x)
        for q in range(20):
            at = slice(q * KLO, (q + 1) * KLO)
            work_ref[0, at, :] = (row_hot * high[q : q + 1]).astype(BF16)
            work_ref[1, at, :] = (row_hot * low[q : q + 1]).astype(BF16)
        part = lax.dot_general(work_ref[0], column_hot, NT, preferred_element_type=F32)
        part += lax.dot_general(work_ref[1], column_hot, NT, preferred_element_type=F32)
        if j == 0:
            total_ref[...] = part
        else:
            total_ref[...] += part


def cells_at(ref, z):
    return [ref[c, z] for c in range(3)]


def first_kernel(
    grad_cells, grad_segs, diag, off, seg_diag, seg_len, device, local, seg, blocks,
    came, slots_out, adjoint_out, rest_out, adjoint_segs_out,
    x, work, slots, lane_hot, table, push, message, off_here, image,
    x_out, x_in, y_out, y_in, column,
    off_sem, send_sem, recv_sem, own_sem, halo_send, halo_recv,
):
    load = pltpu.make_async_copy(off, off_here, off_sem)
    load.start()
    greet()
    exchange = Exchange(message, came, send_sem, recv_sem, own_sem)
    halo = Halo(x_out, x_in, y_out, y_in, halo_send, halo_recv)
    x[0:1, :] = (local[...] + 1).astype(F32)
    x[1:2, :] = seg[...].astype(F32)
    for b in range(2):
        for j in range(3):
            at = 2 + 9 * b + 3 * j
            x[at : at + 3, :] = blocks[b, j]
    rank_and_place(device, x, work, slots)
    active = active_row(seg_len)
    adjoint_segs = [
        active * row for row in solve_rows(seg_matrix(seg_diag), seg_rows(grad_segs))
    ]
    for c in range(3):
        adjoint_segs_out[c : c + 1, :] = adjoint_segs[c]
    seg_slots = slots.at[pl.ds(KLO, KLO)]
    lane_hots(seg_slots, lane_hot)
    seg_gather(adjoint_segs, seg_slots, lane_hot, table, push)
    terms = slot_terms(slots.at[pl.ds(2 * KLO, 18 * KLO)], 0, push, 0)
    packed = jnp.concatenate([slots[0:KLO, :]] + terms, axis=0)
    for h in range(KHI):
        message[:, h, :] = packed[:, ND * h : ND * (h + 1)].T
    greeted()
    exchange.start()
    slots_out[...] = slots[KLO:, :]

    def begin(z, _):
        a = solve_rows(
            [[diag[i, j, z] for j in range(3)] for i in range(3)], cells_at(grad_cells, z)
        )
        for c in range(3):
            adjoint_out[c, z] = a[c]
        return 0

    lax.fori_loop(0, NZ, begin, 0, unroll=2)
    load.wait()
    stencil(lambda z: cells_at(adjoint_out, z), diag, off_here, image, halo, column)
    halo.wait_recv()
    add_rims(image, halo, column)
    for c in range(3):
        rest_out[c] = grad_cells[c] - image[c, 1 : NZ + 1]
    exchange.wait_recv()
    exchange.wait_send()
    halo.wait_send()


def place_slots(index, place_ref, starts):
    row = (index - 1) >> 7
    parts = []
    for b in range(BUCKETS):
        parts.append(((index > 0) & ((row // BROWS) == b)).astype(F32))
    hit = jnp.concatenate(parts, axis=0)
    hit16 = hit.astype(BF16)
    above = (iota((WIDE, WIDE), 0) < iota((WIDE, WIDE), 1)).astype(F32).astype(BF16)
    within = jnp.dot(hit16, above, preferred_element_type=F32)
    totals = jnp.dot(hit16, jnp.ones((WIDE, WIDE), BF16), preferred_element_type=F32)
    r0 = iota((BUCKETS * KLO, BUCKETS * KLO), 0)
    r1 = iota((BUCKETS * KLO, BUCKETS * KLO), 1)
    lower = ((r1 < r0) & ((r1 // KLO) == (r0 // KLO))).astype(F32).astype(BF16)
    earlier = jnp.dot(lower, totals.astype(BF16), preferred_element_type=F32)
    before = within + earlier
    place = jnp.full((KLO, WIDE), -1.0, F32)
    for b in range(BUCKETS):
        at = slice(b * KLO, (b + 1) * KLO)
        base = (starts[b] * CHUNK).astype(F32)
        place = jnp.where(hit[at] > 0, before[at] + base, place)
    place_ref[...] = place.astype(jnp.int32)


def bucket_starts(index):
    row = (index - 1) >> 7
    starts = [jnp.int32(0)]
    for b in range(BUCKETS):
        held = ((index > 0) & ((row // BROWS) == b)).astype(jnp.int32)
        count = jnp.sum(held)
        starts.append(starts[-1] + (count + CHUNK - 1) // CHUNK)
    return starts


def place_hots(place_ref, lane_ref, chunk_ref):
    def body(k, _):
        lanes = pl.ds(pl.multiple_of(k * WIDE, WIDE), WIDE)
        place = place_ref[pl.ds(k, 1), :]
        lane_ref[:, lanes] = one_hot(CHUNK, place & (CHUNK - 1), BF16)
        chunk_ref[:, lanes] = one_hot(CROWS, place >> 9, F32)
        return 0

    lax.fori_loop(0, KLO, body, 0, unroll=2)


def to_places(rows_ref, starts, lane_ref, chunk_ref, out_ref):
    count = len(starts)

    def body(k, _):
        lanes = pl.ds(pl.multiple_of(k * 4 * WIDE, 4 * WIDE), 4 * WIDE)
        chunk = chunk_ref[:, lanes]
        lane = lane_ref[:, lanes]
        left = [[], []]
        for q in range(count):
            value = jnp.concatenate(
                [rows_ref[pl.ds(starts[q] + 4 * k + n, 1), :] for n in range(4)], axis=1
            )
            for p, part in enumerate(halves(value)):
                left[p].append(chunk * part)
        part = lax.dot_general(
            jnp.concatenate(left[0], axis=0).astype(BF16), lane, NT, preferred_element_type=F32
        )
        part += lax.dot_general(
            jnp.concatenate(left[1], axis=0).astype(BF16), lane, NT, preferred_element_type=F32
        )
        out_ref[...] += part
        return 0

    out_ref[...] = jnp.zeros_like(out_ref)
    lax.fori_loop(0, KLO // 4, body, 0)


def from_places(rows_ref, count, lane_ref, chunk_ref, out_ref, starts):
    high, low = halves(rows_ref[...])
    high = high.astype(BF16)
    low = low.astype(BF16)

    def body(k, _):
        lanes = pl.ds(pl.multiple_of(k * 2 * WIDE, 2 * WIDE), 2 * WIDE)
        lane = lane_ref[:, lanes]
        chunk = chunk_ref[:, lanes]
        found = jnp.dot(high, lane, preferred_element_type=F32)
        found += jnp.dot(low, lane, preferred_element_type=F32)
        for q in range(count):
            value = jnp.sum(found[q * CROWS : (q + 1) * CROWS] * chunk, axis=0, keepdims=True)
            for n in range(2):
                out_ref[pl.ds(starts[q] + 2 * k + n, 1), :] = value[:, WIDE * n : WIDE * (n + 1)]
        return 0

    lax.fori_loop(0, KLO // 2, body, 0)


def turn_cells(cells, turned_ref):
    for c in range(3):
        for b in range(BUCKETS):
            block = cells(c, b).T
            high, low = halves(block)
            at = slice(c * CY, (c + 1) * CY)
            turned_ref[b, at, 0:BROWS] = high.astype(BF16)
            turned_ref[b, at, BROWS : 2 * BROWS] = low.astype(BF16)


def chunk_hots(index_ref, j, b):
    index = index_ref[pl.ds(j, 1), :].astype(jnp.int32) - 1
    row = one_hot(BROWS, (index >> 7) - BROWS * b, BF16)
    lane = one_hot(CY, index & 127, F32)
    return row, lane


def gather_chunk(turned, row, lane, out_ref, start, j):
    found = jnp.dot(turned, jnp.concatenate([row, row], axis=0), preferred_element_type=F32)
    for c in range(3):
        out_ref[pl.ds(start + c * CROWS + j, 1), :] = jnp.sum(
            found[c * CY : (c + 1) * CY] * lane, axis=0, keepdims=True
        )


def scatter_chunk(values_ref, start, j, row, lane, total_ref, b):
    high, low = [], []
    for c in range(3):
        one, two = halves(values_ref[pl.ds(start + c * CROWS + j, 1), :])
        high.append(lane * one)
        low.append(lane * two)
    part = lax.dot_general(
        row, jnp.concatenate(high, axis=0).astype(BF16), NT, preferred_element_type=F32
    )
    part += lax.dot_general(
        row, jnp.concatenate(low, axis=0).astype(BF16), NT, preferred_element_type=F32
    )
    total_ref[b] += part


def unpack(came, rows_ref, comps):
    for h in range(KHI):
        rows_ref[0 : comps * KLO, ND * h : ND * (h + 1)] = came[:, h, :].T[0 : comps * KLO]


def second_kernel(
    came, diag, adjoint, rest,
    adjoint_out, message, lane_out, chunk_out, index_out, starts_out,
    rows, place, lane_hot, chunk_hot, ordered, turned, scattered, pulled, pulls,
):
    unpack(came, rows, 4)
    index = rows[0:KLO, :].astype(jnp.int32)
    starts = bucket_starts(index)
    place_slots(index, place, starts)
    place_hots(place, lane_hot, chunk_hot)
    to_places(rows, [q * KLO for q in range(4)], lane_hot, chunk_hot, ordered)
    turn_cells(
        lambda c, b: adjoint[c, 8 * b : 8 * b + 8].reshape(BROWS, CY),
        turned,
    )
    scattered[...] = jnp.zeros_like(scattered)
    pulled[...] = jnp.zeros_like(pulled)
    index_rows = ordered.at[pl.ds(0, CROWS)]
    for b in range(BUCKETS):
        def first(j, _):
            row, lane = chunk_hots(index_rows, j, b)
            gather_chunk(turned[b], row, lane, pulled, 0, j)
            scatter_chunk(ordered, CROWS, j, row, lane, scattered, b)
            return 0

        lax.fori_loop(starts[b], starts[b + 1], first, 0)
    for b in range(BUCKETS):
        def update(n, _):
            z = 8 * b + n
            at = pl.ds(pl.multiple_of(n * CX, CX), CX)
            left = [
                rest[c, z] - scattered[b, at, c * CY : (c + 1) * CY] for c in range(3)
            ]
            step = solve_rows([[diag[i, j, z] for j in range(3)] for i in range(3)], left)
            for c in range(3):
                adjoint_out[c, z] = adjoint[c, z] + step[c]
            return 0

        lax.fori_loop(0, 8, update, 0, unroll=2)
    turn_cells(
        lambda c, b: adjoint_out[c, 8 * b : 8 * b + 8].reshape(BROWS, CY),
        turned,
    )
    for b in range(BUCKETS):
        def second(j, _):
            row, lane = chunk_hots(index_rows, j, b)
            gather_chunk(turned[b], row, lane, pulled, 3 * CROWS, j)
            return 0

        lax.fori_loop(starts[b], starts[b + 1], second, 0)
    pulls[...] = jnp.zeros_like(pulls)
    from_places(
        pulled, 6, lane_hot, chunk_hot, pulls, [q * KLO + (q // 3) * KLO for q in range(6)]
    )
    for h in range(KHI):
        for n in range(2):
            message[:, 2 * h + n, :] = pulls[ND * n : ND * (n + 1), ND * h : ND * (h + 1)].T
    lane_out[...] = lane_hot[...]
    chunk_out[...] = chunk_hot[...]
    index_out[...] = ordered[0:CROWS, :]
    for b in range(BUCKETS + 1):
        starts_out[b] = starts[b]


def seg_image(adjoint, diag, chain, scattered):
    position = iota((1, SEGS), 1) % SEG_MAX
    own = transposed_rows(seg_matrix(diag), adjoint)
    lower = transposed_rows(seg_matrix(chain.at[0]), adjoint)
    upper = transposed_rows(seg_matrix(chain.at[1]), adjoint)
    out = []
    for c in range(3):
        total = own[c] + scattered[c]
        total += jnp.where(position == SEG_MAX - 1, 0.0, pltpu.roll(lower[c], SEGS - 1, 1))
        total += jnp.where(position == 0, 0.0, pltpu.roll(upper[c], 1, 1))
        out.append(total)
    return out


def third_kernel(
    message, grad_cells, adjoint, diag, off,
    grad_segs, adjoint_segs, seg_diag, seg_chain, seg_len, slots,
    came, rest_out, adjoint_segs_out, residual_segs_out,
    pulls_in, push_message, pulls, terms, lane_hot, table, push, off_here, image,
    x_out, x_in, y_out, y_in, column,
    off_sem, send_sem, recv_sem, own_sem, halo_send, halo_recv,
):
    load = pltpu.make_async_copy(off, off_here, off_sem)
    load.start()
    greet()
    pull_exchange = Exchange(message, pulls_in, send_sem.at[0], recv_sem.at[0], own_sem.at[0])
    push_exchange = Exchange(
        push_message, came, send_sem.at[1], recv_sem.at[1], own_sem.at[1]
    )
    halo = Halo(x_out, x_in, y_out, y_in, halo_send, halo_recv)
    seg_slots = slots.at[pl.ds(0, KLO)]
    blocks = slots.at[pl.ds(KLO, 18 * KLO)]
    lane_hots(seg_slots, lane_hot)
    greeted()
    pull_exchange.start()
    load.wait()
    stencil(lambda z: cells_at(adjoint, z), diag, off_here, image, halo, column)
    active = active_row(seg_len)
    grad = seg_rows(grad_segs)
    matrix = seg_matrix(seg_diag)
    before = seg_rows(adjoint_segs)
    pull_exchange.wait_recv()
    for h in range(KHI):
        for n in range(2):
            pulls[ND * n : ND * (n + 1), ND * h : ND * (h + 1)] = pulls_in[:, 2 * h + n, :].T
    for c, term in enumerate(slot_terms(blocks, 1, pulls, 0)):
        terms[c * KLO : (c + 1) * KLO, :] = term
    scattered = seg_scatter(terms, seg_slots, lane_hot, table)
    seen = seg_image(before, seg_diag, seg_chain, scattered)
    step = solve_rows(matrix, [grad[c] - seen[c] for c in range(3)])
    after = [before[c] + active * step[c] for c in range(3)]
    for c in range(3):
        adjoint_segs_out[c : c + 1, :] = after[c]
    seg_gather(after, seg_slots, lane_hot, table, push)
    packed = jnp.concatenate(
        slot_terms(blocks, 0, push, 0) + [jnp.zeros((KLO, WIDE), F32)], axis=0
    )
    for h in range(KHI):
        push_message[:, h, :] = packed[:, ND * h : ND * (h + 1)].T
    push_exchange.start()
    for c, term in enumerate(slot_terms(blocks, 1, pulls, ND)):
        terms[c * KLO : (c + 1) * KLO, :] = term
    scattered = seg_scatter(terms, seg_slots, lane_hot, table)
    seen = seg_image(after, seg_diag, seg_chain, scattered)
    for c in range(3):
        residual_segs_out[c : c + 1, :] = active * (grad[c] - seen[c])
    halo.wait_recv()
    add_rims(image, halo, column)
    for c in range(3):
        rest_out[c] = grad_cells[c] - image[c, 1 : NZ + 1]
    push_exchange.wait_recv()
    pull_exchange.wait_send()
    push_exchange.wait_send()
    halo.wait_send()


def fourth_kernel(
    starts, came, rest, lane_hot, chunk_hot, index_rows, adjoint_segs, residual_segs,
    residual_out, adjoint_segs_out, residual_segs_out,
    rows, ordered, scattered,
):
    adjoint_segs_out[...] = adjoint_segs[...]
    residual_segs_out[...] = residual_segs[...]
    unpack(came, rows, 3)
    to_places(rows, [q * KLO for q in range(3)], lane_hot, chunk_hot, ordered)
    scattered[...] = jnp.zeros_like(scattered)
    for b in range(BUCKETS):
        def body(j, _):
            row, lane = chunk_hots(index_rows, j, b)
            scatter_chunk(ordered, 0, j, row, lane, scattered, b)
            return 0

        lax.fori_loop(starts[b], starts[b + 1], body, 0)
    for b in range(BUCKETS):
        for c in range(3):
            at = slice(8 * b, 8 * b + 8)
            residual_out[c, at] = rest[c, at] - scattered[b, :, c * CY : (c + 1) * CY].reshape(
                8, CX, CY
            )


def shape(*dims, kind=F32):
    return jax.ShapeDtypeStruct(dims, kind)


def vmem(*dims, kind=F32):
    return pltpu.VMEM(dims, kind)


def rim_scratch():
    return [
        vmem(2, 3, NZ, CY),
        vmem(2, 3, NZ, CY),
        vmem(2, 8, ROWS),
        vmem(2, 8, ROWS),
        vmem(ROWS, CY),
    ]


def call(kernel, outs, ins, scratch, number, in_specs=None, limit=58 << 20):
    params = dict(vmem_limit_bytes=limit)
    if number is not None:
        params.update(collective_id=number, has_side_effects=True)
    return pl.pallas_call(
        kernel,
        out_shape=outs,
        in_specs=in_specs or [VMEM] * len(ins),
        out_specs=[VMEM] * len(outs) if not isinstance(outs[-1], tuple) else None,
        scratch_shapes=scratch,
        compiler_params=pltpu.CompilerParams(**params),
        name=kernel.__name__,
    )(*ins)


def shards(
    grad_cells, grad_segs, cell_diag, cell_off, seg_diag, seg_chain, seg_len,
    perf_device, perf_local, perf_seg, perf_blocks,
):
    dma = pltpu.SemaphoreType.DMA
    lens = seg_len.reshape(32, 1)
    cells = shape(3, NZ, CX, CY)
    segs = shape(3, SEGS)
    came, slots, adjoint, rest, adjoint_segs = call(
        first_kernel,
        [shape(ND, KHI, ND), shape(19 * KLO, WIDE), cells, cells, segs],
        [
            grad_cells, grad_segs, cell_diag, cell_off, seg_diag, lens,
            perf_device.reshape(1, PERFS), perf_local.reshape(1, PERFS),
            perf_seg.reshape(1, PERFS), perf_blocks,
        ],
        [
            vmem(24, PERFS),
            vmem(2, 20 * KLO, 512, kind=BF16),
            vmem(20 * KLO, WIDE),
            vmem(128, SLOTS, kind=BF16),
            vmem(24, 256),
            vmem(3 * KLO, WIDE),
            vmem(ND, KHI, ND),
            vmem(6, 3, 3, NZ, CX, CY),
            vmem(3, NZ + 2, CX, CY),
        ]
        + rim_scratch()
        + [dma, dma, dma, dma, dma((4,)), dma((4,))],
        0,
        [VMEM] * 3 + [ANY] + [VMEM] * 6,
    )
    adjoint, message, lane_hot, chunk_hot, index_rows, starts = pl.pallas_call(
        second_kernel,
        out_shape=[
            cells, shape(ND, 4, ND), shape(CHUNK, SLOTS, kind=BF16), shape(CROWS, SLOTS),
            shape(CROWS, CHUNK), shape(8, kind=jnp.int32),
        ],
        in_specs=[VMEM] * 4,
        out_specs=[VMEM] * 5 + [pl.BlockSpec(memory_space=pltpu.SMEM)],
        scratch_shapes=[
            vmem(4 * KLO, WIDE),
            vmem(KLO, WIDE, kind=jnp.int32),
            vmem(CHUNK, SLOTS, kind=BF16),
            vmem(CROWS, SLOTS),
            vmem(4 * CROWS, CHUNK),
            vmem(BUCKETS, 3 * CY, 2 * BROWS, kind=BF16),
            vmem(BUCKETS, BROWS, 3 * CY),
            vmem(6 * CROWS, CHUNK),
            vmem(8 * KLO, WIDE),
        ],
        compiler_params=pltpu.CompilerParams(vmem_limit_bytes=58 << 20),
        name="second_kernel",
    )(came, cell_diag, adjoint, rest)
    came, rest, adjoint_segs, residual_segs = call(
        third_kernel,
        [shape(ND, KHI, ND), cells, segs, segs],
        [
            message, grad_cells, adjoint, cell_diag, cell_off,
            grad_segs, adjoint_segs, seg_diag, seg_chain, lens, slots,
        ],
        [
            vmem(ND, 4, ND),
            vmem(ND, KHI, ND),
            vmem(8 * KLO, WIDE),
            vmem(3 * KLO, WIDE),
            vmem(128, SLOTS, kind=BF16),
            vmem(24, 256),
            vmem(3 * KLO, WIDE),
            vmem(6, 3, 3, NZ, CX, CY),
            vmem(3, NZ + 2, CX, CY),
        ]
        + rim_scratch()
        + [dma, dma((2,)), dma((2,)), dma((2,)), dma((4,)), dma((4,))],
        1,
        [VMEM] * 4 + [ANY] + [VMEM] * 6,
    )
    residual, adjoint_segs, residual_segs = call(
        fourth_kernel,
        [cells, segs, segs],
        [starts, came, rest, lane_hot, chunk_hot, index_rows, adjoint_segs, residual_segs],
        [
            vmem(3 * KLO, WIDE),
            vmem(3 * CROWS, CHUNK),
            vmem(BUCKETS, BROWS, 3 * CY),
        ],
        None,
        [pl.BlockSpec(memory_space=pltpu.SMEM)] + [VMEM] * 7,
    )
    return adjoint, adjoint_segs, residual, residual_segs


def solution(mesh):
    in_specs = (
        P(None, None, "gx", "gy"),
        P(None, ("gx", "gy")),
        P(None, None, None, "gx", "gy"),
        P(None, None, None, None, "gx", "gy"),
        P(None, None, ("gx", "gy")),
        P(None, None, None, ("gx", "gy")),
        P(("gx", "gy")),
        P(("gx", "gy"), None),
        P(("gx", "gy")),
        P(("gx", "gy")),
        P(None, None, None, ("gx", "gy")),
    )
    out_specs = (
        P(None, None, "gx", "gy"),
        P(None, ("gx", "gy")),
        P(None, None, "gx", "gy"),
        P(None, ("gx", "gy")),
    )
    return jax.shard_map(shards, mesh=mesh, in_specs=in_specs, out_specs=out_specs, check_vma=False)
```

time: 946 us -> 116 us (0.12); the launches traced: 931 us -> 116 us
  local copies, waits for them, and re-layouts: 542 us -> 3.94 us
  other arithmetic: 310 us -> 0 us
  Pallas kernels: 0 us -> 111 us
  starting transfers between devices: 74.6 us -> 0 us
    gather x15 -> x0, local copies, waits for them, and re-layouts: 268 us -> none  [the longest x2 79.2 us: couple(): send_pull = cells_flat[:, index_in]]
    scatter-add x8 -> x0, other arithmetic: 195 us -> none  [the longest x2 142 us: couple(): cell_flat = cell_flat.at[:, index_in].add(got_push)]
    pallas_call x0 -> x4, Pallas kernels: none -> 111 us  [the longest x3 77 us: call(): pl.pallas_call(kernel, out_shape=outs, in_specs=in_specs or [VMEM] * len(...]
    add x9 -> x0, other arithmetic: 52.6 us -> none  [the longest x2 34.4 us: shards(): adjoint_cells + apply_inverse(cell_inverse, grad_cells - image_cells)]
    scatter-add x8 -> x0, local copies, waits for them, and re-layouts: 50.7 us -> none  [the longest x2 34.5 us: couple(): cell_out = cell_out.at[:, :-1].add(falling[:, 1:])]
    all_to_all x5 -> x0, starting transfers between devices: 50.5 us -> none  [the longest x2 23.3 us: couple(): lax.all_to_all(send_pull, ('gx', 'gy'), split_axis=1, concat_axis=1, tile...]
    reshape x8 -> x1, local copies, waits for them, and re-layouts: 46.7 us -> 1.34 us  [shards(): lens = seg_len.reshape(32, 1)]
    reduce_sum x6 -> x0, local copies, waits for them, and re-layouts: 42.5 us -> none  [the longest x2 33.7 us: apply_inverse(): return jnp.sum(inverse * vector[None], axis=1)]
  transfers between devices with their start and end apart: 13 -> 0, of which waited for: 1 -> 0; matrix products, arithmetic and copies ran while one was open for 52% -> 0% of each run, Pallas kernels for 0% -> 0%
where the time goes in v1:
time: 116 us
  Pallas kernels  111 us (96%)
  local copies, waits for them, and re-layouts  3.94 us (3%)
    pallas_call x3, Pallas kernels, call(): pl.pallas_call(kernel, out_shape=outs, in_specs=in_specs or [VMEM] * len(...  77 us
    pallas_call x1, Pallas kernels, shards(): pl.pallas_call(second_kernel, out_shape=[cells, shape(ND, 4, ND), shape(C...  34.2 us
    unnamed x4, local copies, waits for them, and re-layouts  2.6 us

profile of v1, /device:TPU:1, one launch (start us, length us, event | category | flops | bytes accessed | tf_op | source)
XLA Modules:
  0.0 115.8 jit_solution(6222843417552117784)
XLA Ops:
  0.6 1.3 %copy.15.seg_len = s32[32,1]{1,0:T(8,128)} copy(s32[32,1]{0,1:T(1,128)} %bitcast.7) | data formatting | bytes 256 | tf_op jit(solution)/shard_map/reshape | solution.py:774
  2.0 1.9 %copy.16.blocks = f32[2,3,3,4096]{3,2,1,0:T(4,128)} copy(f32[2,3,3,4096]{3,0,2,1:T(2,128)} %param.21) | data formatting | bytes 589824 | tf_op args[10]
  3.9 0.0 copy-start
  3.9 30.9 %first_kernel.1 = (f32[128,2,128]{2,1,0:T(2,128)}, f32[608,256]{1,0:T(8,128)}, f32[3,32,16,128]{3,2,1,0:T(8,128)}, f32[3,32,16,128]{3,2,1,0:T(8,128)}, f32[3,1024]{1,0:T(4,128)}) custom-call(f32[3,32,16,128]{3,2,1,0:T(8,128)} %grad_cells.3, f32[3,1024]{1,0:T(4,128)} %grad_segs.3, f32[3,3,32,16,128]{4,3,2,1,0:T(8,128)} %diag.5, ...), custom_call_target="tpu_custom_call" | custom-call | tf_op jit(solution)/shard_map/first_kernel/pallas_call | solution.py:758
  34.8 34.2 %second_kernel.1 = (f32[3,32,16,128]{3,2,1,0:T(8,128)}, f32[128,4,128]{2,1,0:T(4,128)}, bf16[512,8192]{1,0:T(8,128)(2,1)}, f32[24,8192]{1,0:T(8,128)}, f32[24,512]{1,0:T(8,128)}, /*index=5*/s32[8]{0:T(128)}) custom-call(f32[128,2,128]{2,1,0:T(2,128)} %get-tuple-element.22.came, f32[3,3,32,16,128]{4,3,2,1,0:T(8,128)} %diag.5, ...), custom_call_target="tpu_custom_call" | custom-call | tf_op jit(solution)/shard_map/second_kernel/pallas_call | solution.py:801
  69.0 0.0 copy-done
  69.0 0.7 copy.17.seg_chain
  69.7 28.6 %third_kernel.1 = (f32[128,2,128]{2,1,0:T(2,128)}, f32[3,32,16,128]{3,2,1,0:T(8,128)}, f32[3,1024]{1,0:T(4,128)}, f32[3,1024]{1,0:T(4,128)}) custom-call(f32[128,4,128]{2,1,0:T(4,128)} %get-tuple-element.27.message, f32[3,32,16,128]{3,2,1,0:T(8,128)} %grad_cells.3, f32[3,32,16,128]{3,2,1,0:T(8,128)} %get-tuple-element.18.adjoint, ...), custom_call_target="tpu_custom_call" | custom-call | tf_op jit(solution)/shard_map/third_kernel/pallas_call | solution.py:758
  98.3 17.5 %fourth_kernel.1 = (f32[3,32,16,128]{3,2,1,0:T(8,128)}, f32[3,1024]{1,0:T(4,128)}, f32[3,1024]{1,0:T(4,128)}) custom-call(s32[8]{0:T(128)} %get-tuple-element.26.starts, f32[128,2,128]{2,1,0:T(2,128)} %get-tuple-element.30.came, f32[3,32,16,128]{3,2,1,0:T(8,128)} %get-tuple-element.31.rest, bf16[512,8192]{1,0:T(8,128)(2,1)} %get-tuple-element.32.lane_hot, ...), custom_call_target="tpu_custom_call" | custom-call | tf_op jit(solution)/shard_map/fourth_kernel/pallas_call | solution.py:758
Async XLA Ops:
  3.9 65.1 %copy-start = (f32[2,3,3,1024]{3,0,2,1:T(2,128)S(1)}, f32[2,3,3,1024]{3,0,2,1:T(2,128)}, u32[]{:S(2)}) copy-start(f32[2,3,3,1024]{3,0,2,1:T(2,128)} %param.16) | copy-start | bytes 221188

commit v2 on v1

v2 whole, which is shorter than its diff:
```python
import jax
import jax.numpy as jnp
from jax import lax
from jax.experimental import pallas as pl
from jax.experimental.pallas import tpu as pltpu
from jax.sharding import PartitionSpec as P

MESH = pl.DeviceIdType.MESH
F32 = jnp.float32
BF16 = jnp.bfloat16
NT = (((1,), (1,)), ((), ()))
GX = 8
GY = 16
ND = GX * GY
NZ = 32
CX = 16
CY = 128
ROWS = NZ * CX
SEGS = 1024
SEG_MAX = 32
PERFS = 4096
KLO = 32
KHI = 2
WIDE = KHI * ND
SLOTS = KLO * WIDE
BUCKETS = 4
BROWS = ROWS // BUCKETS
CHUNK = 512
LANES = 256
CROWS = 40
SPARE = CROWS * LANES // CHUNK - 1
VMEM = pl.BlockSpec(memory_space=pltpu.VMEM)
ANY = pl.BlockSpec(memory_space=pl.ANY)


def rounded(x):
    return x.astype(BF16).astype(F32)


def halves(x):
    high = rounded(x)
    return high, x - high


def iota(shape, dim):
    return lax.broadcasted_iota(jnp.int32, shape, dim)


def one_hot(count, row, kind):
    hit = iota((count, row.shape[1]), 0) == row
    return hit.astype(F32).astype(kind)


def inverse_rows(matrix):
    cofactor = [
        [
            matrix[(i + 1) % 3][(j + 1) % 3] * matrix[(i + 2) % 3][(j + 2) % 3]
            - matrix[(i + 1) % 3][(j + 2) % 3] * matrix[(i + 2) % 3][(j + 1) % 3]
            for j in range(3)
        ]
        for i in range(3)
    ]
    determinant = (
        matrix[0][0] * cofactor[0][0]
        + matrix[0][1] * cofactor[0][1]
        + matrix[0][2] * cofactor[0][2]
    )
    return cofactor, 1.0 / determinant


def solve_rows(matrix, vector):
    cofactor, scale = inverse_rows(matrix)
    return [
        (cofactor[i][0] * vector[0] + cofactor[i][1] * vector[1] + cofactor[i][2] * vector[2])
        * scale
        for i in range(3)
    ]


def transposed_rows(matrix, vector):
    return [
        matrix[0][i] * vector[0] + matrix[1][i] * vector[1] + matrix[2][i] * vector[2]
        for i in range(3)
    ]


def seg_rows(ref):
    return [ref[j : j + 1, :] for j in range(3)]


def seg_matrix(ref):
    return [[ref[i, j : j + 1, :] for j in range(3)] for i in range(3)]


def active_row(seg_len_ref):
    square = iota((32, 32), 0) == iota((32, 32), 1)
    lens = jnp.sum(jnp.where(square, seg_len_ref[...].astype(F32), 0.0), axis=1, keepdims=True)
    lanes = iota((32, SEGS), 1)
    mine = (lanes // SEG_MAX) == iota((32, SEGS), 0)
    below = (lanes % SEG_MAX).astype(F32) < lens
    return jnp.sum(jnp.where(mine & below, 1.0, 0.0), axis=0, keepdims=True)


def four_rows(ref, start, k):
    return jnp.concatenate([ref[pl.ds(start + 4 * k + n, 1), :] for n in range(4)], axis=1)


def put_four_rows(ref, start, k, value):
    for n in range(4):
        ref[pl.ds(start + 4 * k + n, 1), :] = value[:, WIDE * n : WIDE * (n + 1)]


def four_lanes(k):
    return pl.ds(pl.multiple_of(k * 4 * WIDE, 4 * WIDE), 4 * WIDE)


def seg_gather(values, seg_slots, lane_hot_ref, table_ref, out_ref):
    for c in range(3):
        for p, part in enumerate(halves(values[c])):
            for h in range(8):
                at = p * 24 + c * 8 + h
                table_ref[at : at + 1, :] = part[:, 128 * h : 128 * (h + 1)]
    table = table_ref[...].astype(BF16)

    def body(k, _):
        found = jnp.dot(table, lane_hot_ref[:, four_lanes(k)], preferred_element_type=F32)
        found = found[:24] + found[24:]
        high = four_rows(seg_slots, 0, k).astype(jnp.int32) >> 7
        pick = (iota((8, 4 * WIDE), 0) == high).astype(F32)
        for c in range(3):
            value = jnp.sum(found[8 * c : 8 * c + 8] * pick, axis=0, keepdims=True)
            put_four_rows(out_ref, c * KLO, k, value)
        return 0

    lax.fori_loop(0, KLO // 4, body, 0, unroll=2)


def seg_scatter(values_ref, seg_slots, lane_hot_ref, table_ref):
    def body(k, total):
        high = four_rows(seg_slots, 0, k).astype(jnp.int32) >> 7
        pick = (iota((8, 4 * WIDE), 0) == high).astype(F32)
        right = []
        for c in range(3):
            right += [pick * part for part in halves(four_rows(values_ref, c * KLO, k))]
        return total + lax.dot_general(
            lane_hot_ref[:, four_lanes(k)],
            jnp.concatenate(right, axis=0).astype(BF16),
            NT,
            preferred_element_type=F32,
        )

    total = lax.fori_loop(0, KLO // 4, body, jnp.zeros((128, 48), F32), unroll=2)
    turned = jnp.concatenate([total, jnp.zeros((128, 80), F32)], axis=1).T
    rows = []
    for c in range(3):
        table_ref[0:8, :] = turned[16 * c : 16 * c + 8] + turned[16 * c + 8 : 16 * c + 16]
        rows.append(jnp.concatenate([table_ref[h : h + 1, :] for h in range(8)], axis=1))
    return rows


def lane_hots(seg_slots, lane_hot_ref):
    def body(k, _):
        low = four_rows(seg_slots, 0, k).astype(jnp.int32) & 127
        lane_hot_ref[:, four_lanes(k)] = one_hot(128, low, BF16)
        return 0

    lax.fori_loop(0, KLO // 4, body, 0)


def slot_terms(blocks, rows_ref, start):
    vector = [rows_ref[start + c * KLO : start + (c + 1) * KLO, :] for c in range(3)]
    out = []
    for i in range(3):
        total = None
        for j in range(3):
            at = (j * 3 + i) * KLO
            term = blocks[at : at + KLO, :] * vector[j]
            total = term if total is None else total + term
        out.append(total)
    return out


def everyone(act):
    gx = lax.axis_index("gx")
    gy = lax.axis_index("gy")
    me = gx * GY + gy

    def body(i, _):
        other = lax.rem(me + i, ND)
        act(other, (other // GY, lax.rem(other, GY)))
        return 0

    lax.fori_loop(1, ND, body, 0)


def greet():
    barrier = pltpu.get_barrier_semaphore()
    everyone(
        lambda other, place: pl.semaphore_signal(
            barrier, inc=1, device_id=place, device_id_type=MESH
        )
    )


def greeted():
    pl.semaphore_wait(pltpu.get_barrier_semaphore(), ND - 1)


class Exchange:
    def __init__(self, source, target, send_sem, recv_sem, own_sem):
        self.source, self.target = source, target
        self.send_sem, self.recv_sem, self.own_sem = send_sem, recv_sem, own_sem
        self.me = lax.axis_index("gx") * GY + lax.axis_index("gy")

    def own(self):
        return pltpu.make_async_copy(
            self.source.at[self.me], self.target.at[self.me], self.own_sem
        )

    def whole(self):
        return pltpu.make_async_remote_copy(
            src_ref=self.source.at[pl.ds(0, ND - 1)],
            dst_ref=self.target.at[pl.ds(0, ND - 1)],
            send_sem=self.send_sem,
            recv_sem=self.recv_sem,
            device_id=(lax.axis_index("gx"), lax.axis_index("gy")),
            device_id_type=MESH,
        )

    def start(self):
        self.own().start()
        everyone(
            lambda other, place: pltpu.make_async_remote_copy(
                src_ref=self.source.at[other],
                dst_ref=self.target.at[self.me],
                send_sem=self.send_sem,
                recv_sem=self.recv_sem,
                device_id=place,
                device_id_type=MESH,
            ).start()
        )

    def wait_recv(self):
        self.own().wait()
        self.whole().wait_recv()

    def wait_send(self):
        self.whole().wait_send()


class Halo:
    def __init__(self, x_out, x_in, y_out, y_in, send_sem, recv_sem):
        gx = lax.axis_index("gx")
        gy = lax.axis_index("gy")
        places = [
            (lax.rem(gx + 1, GX), gy),
            (lax.rem(gx + GX - 1, GX), gy),
            (gx, lax.rem(gy + 1, GY)),
            (gx, lax.rem(gy + GY - 1, GY)),
        ]
        pairs = [(x_out, x_in, 0), (x_out, x_in, 1), (y_out, y_in, 0), (y_out, y_in, 1)]
        self.copies = [
            pltpu.make_async_remote_copy(
                src_ref=a.at[n],
                dst_ref=b.at[n],
                send_sem=send_sem.at[at],
                recv_sem=recv_sem.at[at],
                device_id=place,
                device_id_type=MESH,
            )
            for at, ((a, b, n), place) in enumerate(zip(pairs, places))
        ]
        self.x_out, self.x_in, self.y_out, self.y_in = x_out, x_in, y_out, y_in

    def start(self):
        for copy in self.copies:
            copy.start()

    def wait_recv(self):
        for copy in self.copies:
            copy.wait_recv()

    def wait_send(self):
        for copy in self.copies:
            copy.wait_send()


def stencil(adjoint, diag_ref, off_ref, image_ref, halo, column_ref):
    for c in range(3):
        image_ref[c] = jnp.zeros((NZ + 2, CX, CY), F32)
    rows = iota((CX, CY), 0)
    lanes = iota((CX, CY), 1)

    def body(z, _):
        a = adjoint(z)
        own = transposed_rows([[diag_ref[j, i, z] for i in range(3)] for j in range(3)], a)
        moved = [
            transposed_rows([[off_ref[e, j, i, z] for i in range(3)] for j in range(3)], a)
            for e in range(6)
        ]
        columns = jnp.zeros((CX, CY), F32)
        for c in range(3):
            total = own[c]
            halo.x_out[0, c, pl.ds(z, 1), :] = moved[0][c][CX - 1 : CX]
            halo.x_out[1, c, pl.ds(z, 1), :] = moved[1][c][0:1]
            total += jnp.where(rows == 0, 0.0, pltpu.roll(moved[0][c], 1, 0))
            total += jnp.where(rows == CX - 1, 0.0, pltpu.roll(moved[1][c], CX - 1, 0))
            total += jnp.where(lanes == 0, 0.0, pltpu.roll(moved[2][c], 1, 1))
            total += jnp.where(lanes == CY - 1, 0.0, pltpu.roll(moved[3][c], CY - 1, 1))
            columns = jnp.where(lanes == c, pltpu.roll(moved[2][c], 1 + c, 1), columns)
            columns = jnp.where(lanes == 8 + c, pltpu.roll(moved[3][c], 8 + c, 1), columns)
            image_ref[c, z + 1] += total
            image_ref[c, z + 2] += moved[4][c]
            image_ref[c, z] += moved[5][c]
        column_ref[pl.ds(pl.multiple_of(z * CX, CX), CX), :] = columns
        return 0

    lax.fori_loop(0, NZ, body, 0, unroll=2)
    turned = column_ref[...].T
    halo.y_out[0] = turned[0:8]
    halo.y_out[1] = turned[8:16]
    halo.start()


def add_rims(image_ref, halo, column_ref):
    gx = lax.axis_index("gx")
    gy = lax.axis_index("gy")
    first_x = jnp.where(gx > 0, 1.0, 0.0)
    last_x = jnp.where(gx < GX - 1, 1.0, 0.0)
    first_y = jnp.where(gy > 0, 1.0, 0.0)
    last_y = jnp.where(gy < GY - 1, 1.0, 0.0)
    came = jnp.concatenate(
        [halo.y_in[0] * first_y, halo.y_in[1] * last_y, jnp.zeros((CY - 16, ROWS), F32)], axis=0
    )
    column_ref[...] = came.T
    rows = iota((CX, CY), 0)
    lanes = iota((CX, CY), 1)

    def body(z, _):
        columns = column_ref[pl.ds(pl.multiple_of(z * CX, CX), CX), :]
        for c in range(3):
            low = halo.x_in[0, c, pl.ds(z, 1), :] * first_x
            high = halo.x_in[1, c, pl.ds(z, 1), :] * last_x
            total = jnp.where(rows == 0, low, 0.0) + jnp.where(rows == CX - 1, high, 0.0)
            left = columns if c == 0 else pltpu.roll(columns, CY - c, 1)
            total += jnp.where(lanes == 0, left, 0.0)
            right = pltpu.roll(columns, CY - 1 - 8 - c, 1)
            total += jnp.where(lanes == CY - 1, right, 0.0)
            image_ref[c, z + 1] += total
        return 0

    lax.fori_loop(0, NZ, body, 0, unroll=2)


def rank_rows(device_ref, column_ref, row_ref):
    above = (iota((256, 256), 0) < iota((256, 256), 1)).astype(F32).astype(BF16)
    ones = jnp.ones((256, 256), BF16)
    carry = jnp.zeros((ND, 256), F32)
    for j in range(PERFS // 256):
        at = slice(256 * j, 256 * (j + 1))
        target = device_ref[:, at]
        hit = one_hot(ND, target, F32)
        hit16 = hit.astype(BF16)
        before = jnp.dot(hit16, above, preferred_element_type=F32) + carry
        carry = carry + jnp.dot(hit16, ones, preferred_element_type=F32)
        rank = jnp.sum(before * hit, axis=0, keepdims=True).astype(jnp.int32)
        column_ref[:, at] = one_hot(WIDE, target + ND * (rank >> 5), BF16)
        row_ref[:, at] = one_hot(KLO, rank & (KLO - 1), F32)


def place_rows(row, count, column_ref, row_ref, work_ref, total_ref, out_ref):
    size = count * KLO
    for j in range(PERFS // 512):
        at = slice(512 * j, 512 * (j + 1))
        row_hot = row_ref[:, at]
        for q in range(count):
            for p, part in enumerate(halves(row(q, at))):
                put = p * size + q * KLO
                work_ref[put : put + KLO, :] = (row_hot * part).astype(BF16)
        part = lax.dot_general(
            work_ref[0 : 2 * size, :], column_ref[:, at], NT, preferred_element_type=F32
        )
        if j == 0:
            total_ref[0 : 2 * size, :] = part
        else:
            total_ref[0 : 2 * size, :] += part
    out_ref[...] = total_ref[0:size, :] + total_ref[size : 2 * size, :]


def cells_at(ref, z):
    return [ref[c, z] for c in range(3)]


def first_kernel(
    grad_cells, grad_segs, diag, off, seg_diag, seg_len, device, local, seg, blocks,
    came, seg_slots, push_blocks, pull_blocks, adjoint_out, rest_out, adjoint_segs_out,
    column_hot, row_hot, work, total, slots, lane_hot, table, push, message,
    off_here, diag_here, grad_here, image,
    x_out, x_in, y_out, y_in, column,
    load_sem, send_sem, recv_sem, own_sem, halo_send, halo_recv,
):
    loads = [
        pltpu.make_async_copy(a, b, load_sem.at[n])
        for n, (a, b) in enumerate(
            [(diag, diag_here), (grad_cells, grad_here), (off, off_here)]
        )
    ]
    for load in loads:
        load.start()
    greet()
    exchange = Exchange(message, came, send_sem, recv_sem, own_sem)
    halo = Halo(x_out, x_in, y_out, y_in, halo_send, halo_recv)
    rank_rows(device, column_hot, row_hot)

    def first_rows(q, at):
        if q == 0:
            return (local[:, at] + 1).astype(F32)
        if q == 1:
            return seg[:, at].astype(F32)
        return blocks[(q - 2) // 3, (q - 2) % 3, 0:1, at]

    place_rows(first_rows, 11, column_hot, row_hot, work, total, slots)
    active = active_row(seg_len)
    adjoint_segs = [
        active * row for row in solve_rows(seg_matrix(seg_diag), seg_rows(grad_segs))
    ]
    for c in range(3):
        adjoint_segs_out[c : c + 1, :] = adjoint_segs[c]
    seg_slots[...] = slots[KLO : 2 * KLO, :]
    push_blocks[...] = slots[2 * KLO :, :]
    lane_hots(seg_slots, lane_hot)
    seg_gather(adjoint_segs, seg_slots, lane_hot, table, push)
    terms = slot_terms(push_blocks, push, 0)
    packed = jnp.concatenate([slots[0:KLO, :]] + terms, axis=0)
    for h in range(KHI):
        message[:, h, :] = packed[:, ND * h : ND * (h + 1)].T
    greeted()
    exchange.start()
    loads[0].wait()
    loads[1].wait()

    def begin(z, _):
        a = solve_rows(
            [[diag_here[i, j, z] for j in range(3)] for i in range(3)], cells_at(grad_here, z)
        )
        for c in range(3):
            adjoint_out[c, z] = a[c]
        return 0

    lax.fori_loop(0, NZ, begin, 0, unroll=2)
    loads[2].wait()
    stencil(lambda z: cells_at(adjoint_out, z), diag_here, off_here, image, halo, column)
    place_rows(
        lambda q, at: blocks[q // 3, q % 3, 1:2, at],
        9, column_hot, row_hot, work, total, pull_blocks,
    )
    halo.wait_recv()
    add_rims(image, halo, column)
    for c in range(3):
        rest_out[c] = grad_here[c] - image[c, 1 : NZ + 1]
    exchange.wait_recv()
    exchange.wait_send()
    halo.wait_send()


def place_slots(index, place_ref, starts):
    row = (index - 1) >> 7
    parts = []
    for b in range(BUCKETS):
        parts.append(((index > 0) & ((row // BROWS) == b)).astype(F32))
    hit = jnp.concatenate(parts, axis=0)
    hit16 = hit.astype(BF16)
    above = (iota((WIDE, WIDE), 0) < iota((WIDE, WIDE), 1)).astype(F32).astype(BF16)
    within = jnp.dot(hit16, above, preferred_element_type=F32)
    totals = jnp.dot(hit16, jnp.ones((WIDE, WIDE), BF16), preferred_element_type=F32)
    r0 = iota((BUCKETS * KLO, BUCKETS * KLO), 0)
    r1 = iota((BUCKETS * KLO, BUCKETS * KLO), 1)
    lower = ((r1 < r0) & ((r1 // KLO) == (r0 // KLO))).astype(F32).astype(BF16)
    earlier = jnp.dot(lower, totals.astype(BF16), preferred_element_type=F32)
    before = within + earlier
    place = jnp.full((KLO, WIDE), -1.0, F32)
    for b in range(BUCKETS):
        at = slice(b * KLO, (b + 1) * KLO)
        base = (starts[b] * CHUNK).astype(F32)
        place = jnp.where(hit[at] > 0, before[at] + base, place)
    place_ref[...] = place.astype(jnp.int32)


def bucket_starts(index):
    row = (index - 1) >> 7
    starts = [jnp.int32(0)]
    for b in range(BUCKETS):
        held = ((index > 0) & ((row // BROWS) == b)).astype(jnp.int32)
        count = jnp.sum(held)
        starts.append(starts[-1] + (count + CHUNK - 1) // CHUNK)
    return starts


def place_hots(place_ref, lane_ref, chunk_ref):
    def body(k, _):
        place = four_rows(place_ref, 0, k)
        lane_ref[:, four_lanes(k)] = one_hot(LANES, place & (LANES - 1), BF16)
        chunk_ref[:, four_lanes(k)] = one_hot(CROWS, place >> 8, F32)
        return 0

    lax.fori_loop(0, KLO // 4, body, 0)


def to_places(rows_ref, count, lane_ref, chunk_ref, total_ref, out_ref):
    size = count * CROWS

    def body(k, _):
        chunk = chunk_ref[:, four_lanes(k)]
        left = [[], []]
        for q in range(count):
            for p, part in enumerate(halves(four_rows(rows_ref, q * KLO, k))):
                left[p].append(chunk * part)
        total_ref[0 : 2 * size, :] += lax.dot_general(
            jnp.concatenate(left[0] + left[1], axis=0).astype(BF16),
            lane_ref[:, four_lanes(k)],
            NT,
            preferred_element_type=F32,
        )
        return 0

    total_ref[...] = jnp.zeros_like(total_ref)
    lax.fori_loop(0, KLO // 4, body, 0, unroll=2)
    out_ref[...] = total_ref[0:size, :] + total_ref[size : 2 * size, :]


def from_places(rows_ref, count, lane_ref, chunk_ref, out_ref, starts):
    size = count * CROWS
    both = jnp.concatenate(halves(rows_ref[...]), axis=0).astype(BF16)

    def body(k, _):
        chunk = chunk_ref[:, four_lanes(k)]
        found = jnp.dot(both, lane_ref[:, four_lanes(k)], preferred_element_type=F32)
        for q in range(count):
            at = q * CROWS
            value = found[at : at + CROWS] + found[size + at : size + at + CROWS]
            put_four_rows(
                out_ref, starts[q], k, jnp.sum(value * chunk, axis=0, keepdims=True)
            )
        return 0

    lax.fori_loop(0, KLO // 4, body, 0, unroll=2)


def turn_cells(cells, turned_ref):
    for c in range(3):
        for b in range(BUCKETS):
            block = cells(c, b).T
            high, low = halves(block)
            at = slice(c * CY, (c + 1) * CY)
            turned_ref[b, at, 0:BROWS] = high.astype(BF16)
            turned_ref[b, at, BROWS : 2 * BROWS] = low.astype(BF16)


def two_rows(ref, start, j):
    return jnp.concatenate([ref[pl.ds(start + 2 * j + n, 1), :] for n in range(2)], axis=1)


def chunk_hots(index_ref, j, b):
    index = two_rows(index_ref, 0, j).astype(jnp.int32) - 1
    row = one_hot(BROWS, (index >> 7) - BROWS * b, BF16)
    lane = one_hot(CY, index & 127, F32)
    return row, lane


def gather_chunk(turned, row, lane, out_ref, start, j):
    found = jnp.dot(turned, jnp.concatenate([row, row], axis=0), preferred_element_type=F32)
    for c in range(3):
        value = jnp.sum(found[c * CY : (c + 1) * CY] * lane, axis=0, keepdims=True)
        for n in range(2):
            out_ref[pl.ds(start + c * CROWS + 2 * j + n, 1), :] = value[
                :, LANES * n : LANES * (n + 1)
            ]


def scatter_chunk(values_ref, start, j, row, lane, total_ref, b):
    high, low = [], []
    for c in range(3):
        one, two = halves(two_rows(values_ref, start + c * CROWS, j))
        high.append(lane * one)
        low.append(lane * two)
    part = lax.dot_general(
        jnp.concatenate(high + low, axis=0).astype(BF16), row, NT, preferred_element_type=F32
    )
    total_ref[b] += part[: 3 * CY] + part[3 * CY :]


def each_chunk(starts, act):
    counts = [starts[b + 1] - starts[b] for b in range(BUCKETS)]
    steps = counts[0]
    for count in counts[1:]:
        steps = jnp.maximum(steps, count)

    def body(t, _):
        for b in range(BUCKETS):
            act(b, jnp.where(t < counts[b], starts[b] + t, SPARE))
        return 0

    lax.fori_loop(0, steps, body, 0)


def scattered_cells(total_ref, b, c):
    return total_ref[b, c * CY : (c + 1) * CY, :].T.reshape(NZ // BUCKETS, CX, CY)


def unpack(came, rows_ref, comps):
    for h in range(KHI):
        rows_ref[0 : comps * KLO, ND * h : ND * (h + 1)] = came[:, h, :].T[0 : comps * KLO]


def second_kernel(
    came, diag, adjoint, rest,
    adjoint_out, pulled, index_out, place, starts_out,
    rows, lane_hot, chunk_hot, total, ordered, turned, scattered,
    diag_here, adjoint_here, rest_here, load_sem,
):
    loads = [
        pltpu.make_async_copy(a, b, load_sem.at[n])
        for n, (a, b) in enumerate(
            [(adjoint, adjoint_here), (diag, diag_here), (rest, rest_here)]
        )
    ]
    for load in loads:
        load.start()
    unpack(came, rows, 4)
    index = rows[0:KLO, :].astype(jnp.int32)
    starts = bucket_starts(index)
    place_slots(index, place, starts)
    place_hots(place, lane_hot, chunk_hot)
    to_places(rows, 4, lane_hot, chunk_hot, total, ordered)
    loads[0].wait()
    turn_cells(
        lambda c, b: adjoint_here[c, 8 * b : 8 * b + 8].reshape(BROWS, CY),
        turned,
    )
    scattered[...] = jnp.zeros_like(scattered)
    pulled[...] = jnp.zeros_like(pulled)
    index_rows = ordered.at[pl.ds(0, CROWS)]

    def first(b, j):
        row, lane = chunk_hots(index_rows, j, b)
        gather_chunk(turned[b], row, lane, pulled, 0, j)
        scatter_chunk(ordered, CROWS, j, row, lane, scattered, b)

    each_chunk(starts, first)
    loads[1].wait()
    loads[2].wait()
    for b in range(BUCKETS):
        for c in range(3):
            at = slice(8 * b, 8 * b + 8)
            rest_here[c, at] = rest_here[c, at] - scattered_cells(scattered, b, c)

    def update(z, _):
        step = solve_rows(
            [[diag_here[i, j, z] for j in range(3)] for i in range(3)], cells_at(rest_here, z)
        )
        for c in range(3):
            adjoint_out[c, z] = adjoint_here[c, z] + step[c]
        return 0

    lax.fori_loop(0, NZ, update, 0, unroll=2)
    turn_cells(
        lambda c, b: adjoint_out[c, 8 * b : 8 * b + 8].reshape(BROWS, CY),
        turned,
    )

    def second(b, j):
        row, lane = chunk_hots(index_rows, j, b)
        gather_chunk(turned[b], row, lane, pulled, 3 * CROWS, j)

    each_chunk(starts, second)
    index_out[...] = ordered[0:CROWS, :]
    for b in range(BUCKETS + 1):
        starts_out[b] = starts[b]


def seg_image(adjoint, diag, chain, scattered):
    position = iota((1, SEGS), 1) % SEG_MAX
    own = transposed_rows(seg_matrix(diag), adjoint)
    lower, upper = [
        transposed_rows(
            [[chain[i, j, n : n + 1, :] for j in range(3)] for i in range(3)], adjoint
        )
        for n in range(2)
    ]
    out = []
    for c in range(3):
        total = own[c] + scattered[c]
        total += jnp.where(position == SEG_MAX - 1, 0.0, pltpu.roll(lower[c], SEGS - 1, 1))
        total += jnp.where(position == 0, 0.0, pltpu.roll(upper[c], 1, 1))
        out.append(total)
    return out


def third_kernel(
    pulled, place, grad_cells, adjoint, diag, off,
    grad_segs, adjoint_segs, seg_diag, seg_chain, seg_len, seg_slots, push_blocks, pull_blocks,
    ordered, rest_out, adjoint_segs_out, residual_segs_out,
    place_lane, place_chunk, total, message, pulls_in, push_message, came,
    pulls, terms, lane_hot, table, push, off_here, diag_here, grad_here, adjoint_here, image,
    x_out, x_in, y_out, y_in, column,
    load_sem, send_sem, recv_sem, own_sem, halo_send, halo_recv,
):
    greet()
    loads = [
        pltpu.make_async_copy(a, b, load_sem.at[n])
        for n, (a, b) in enumerate(
            [
                (adjoint, adjoint_here), (diag, diag_here),
                (off, off_here), (grad_cells, grad_here),
            ]
        )
    ]
    for load in loads:
        load.start()
    pull_exchange = Exchange(message, pulls_in, send_sem.at[0], recv_sem.at[0], own_sem.at[0])
    push_exchange = Exchange(
        push_message, came, send_sem.at[1], recv_sem.at[1], own_sem.at[1]
    )
    halo = Halo(x_out, x_in, y_out, y_in, halo_send, halo_recv)
    place_hots(place, place_lane, place_chunk)
    pulls[...] = jnp.zeros_like(pulls)
    from_places(
        pulled, 6, place_lane, place_chunk, pulls,
        [q * KLO + (q // 3) * KLO for q in range(6)],
    )
    for h in range(KHI):
        for n in range(2):
            message[:, 2 * h + n, :] = pulls[ND * n : ND * (n + 1), ND * h : ND * (h + 1)].T
    greeted()
    pull_exchange.start()
    for load in loads[:3]:
        load.wait()
    stencil(lambda z: cells_at(adjoint_here, z), diag_here, off_here, image, halo, column)
    lane_hots(seg_slots, lane_hot)
    active = active_row(seg_len)
    grad = seg_rows(grad_segs)
    matrix = seg_matrix(seg_diag)
    before = seg_rows(adjoint_segs)
    pull_exchange.wait_recv()
    for h in range(KHI):
        for n in range(2):
            pulls[ND * n : ND * (n + 1), ND * h : ND * (h + 1)] = pulls_in[:, 2 * h + n, :].T
    for c, term in enumerate(slot_terms(pull_blocks, pulls, 0)):
        terms[c * KLO : (c + 1) * KLO, :] = term
    scattered = seg_scatter(terms, seg_slots, lane_hot, table)
    seen = seg_image(before, seg_diag, seg_chain, scattered)
    step = solve_rows(matrix, [grad[c] - seen[c] for c in range(3)])
    after = [before[c] + active * step[c] for c in range(3)]
    for c in range(3):
        adjoint_segs_out[c : c + 1, :] = after[c]
    seg_gather(after, seg_slots, lane_hot, table, push)
    packed = jnp.concatenate(
        slot_terms(push_blocks, push, 0) + [jnp.zeros((KLO, WIDE), F32)], axis=0
    )
    for h in range(KHI):
        push_message[:, h, :] = packed[:, ND * h : ND * (h + 1)].T
    push_exchange.start()
    for c, term in enumerate(slot_terms(pull_blocks, pulls, ND)):
        terms[c * KLO : (c + 1) * KLO, :] = term
    scattered = seg_scatter(terms, seg_slots, lane_hot, table)
    seen = seg_image(after, seg_diag, seg_chain, scattered)
    for c in range(3):
        residual_segs_out[c : c + 1, :] = active * (grad[c] - seen[c])
    halo.wait_recv()
    add_rims(image, halo, column)
    loads[3].wait()
    for c in range(3):
        rest_out[c] = grad_here[c] - image[c, 1 : NZ + 1]
    push_exchange.wait_recv()
    unpack(came, pulls, 3)
    to_places(pulls, 3, place_lane, place_chunk, total, ordered)
    pull_exchange.wait_send()
    push_exchange.wait_send()
    halo.wait_send()


def fourth_kernel(
    starts, ordered, rest, index_rows, adjoint_segs, residual_segs,
    residual_out, adjoint_segs_out, residual_segs_out,
    scattered,
):
    adjoint_segs_out[...] = adjoint_segs[...]
    residual_segs_out[...] = residual_segs[...]
    scattered[...] = jnp.zeros_like(scattered)

    def act(b, j):
        row, lane = chunk_hots(index_rows, j, b)
        scatter_chunk(ordered, 0, j, row, lane, scattered, b)

    each_chunk([starts[b] for b in range(BUCKETS + 1)], act)
    for b in range(BUCKETS):
        for c in range(3):
            at = slice(8 * b, 8 * b + 8)
            residual_out[c, at] = rest[c, at] - scattered_cells(scattered, b, c)


def shape(*dims, kind=F32):
    return jax.ShapeDtypeStruct(dims, kind)


def vmem(*dims, kind=F32):
    return pltpu.VMEM(dims, kind)


def rim_scratch():
    return [
        vmem(2, 3, NZ, CY),
        vmem(2, 3, NZ, CY),
        vmem(2, 8, ROWS),
        vmem(2, 8, ROWS),
        vmem(ROWS, CY),
    ]


def call(kernel, outs, ins, scratch, number=None, in_specs=None, out_specs=None):
    params = dict(vmem_limit_bytes=58 << 20)
    if number is not None:
        params.update(collective_id=number, has_side_effects=True)
    return pl.pallas_call(
        kernel,
        out_shape=outs,
        in_specs=in_specs or [VMEM] * len(ins),
        out_specs=out_specs or [VMEM] * len(outs),
        scratch_shapes=scratch,
        compiler_params=pltpu.CompilerParams(**params),
        name=kernel.__name__,
    )(*ins)


def shards(
    grad_cells, grad_segs, cell_diag, cell_off, seg_diag, seg_chain, seg_len,
    perf_device, perf_local, perf_seg, perf_blocks,
):
    dma = pltpu.SemaphoreType.DMA
    smem = pl.BlockSpec(memory_space=pltpu.SMEM)
    lens = seg_len.reshape(1, 32)
    chain = seg_chain.transpose(1, 2, 0, 3)
    cells = shape(3, NZ, CX, CY)
    segs = shape(3, SEGS)
    tile = vmem(3, NZ, CX, CY)
    diag_tile = vmem(3, 3, NZ, CX, CY)
    off_tile = vmem(6, 3, 3, NZ, CX, CY)
    image = vmem(3, NZ + 2, CX, CY)
    came, seg_slots, push_blocks, pull_blocks, adjoint, rest, adjoint_segs = call(
        first_kernel,
        [
            shape(ND, KHI, ND), shape(KLO, WIDE), shape(9 * KLO, WIDE), shape(9 * KLO, WIDE),
            cells, cells, segs,
        ],
        [
            grad_cells, grad_segs, cell_diag, cell_off, seg_diag, lens,
            perf_device.reshape(1, PERFS), perf_local.reshape(1, PERFS),
            perf_seg.reshape(1, PERFS), perf_blocks.transpose(1, 2, 0, 3),
        ],
        [
            vmem(WIDE, PERFS, kind=BF16),
            vmem(KLO, PERFS),
            vmem(22 * KLO, 512, kind=BF16),
            vmem(22 * KLO, WIDE),
            vmem(11 * KLO, WIDE),
            vmem(128, SLOTS, kind=BF16),
            vmem(48, 128),
            vmem(3 * KLO, WIDE),
            vmem(ND, KHI, ND),
            off_tile,
            diag_tile,
            tile,
            image,
        ]
        + rim_scratch()
        + [dma((3,)), dma, dma, dma, dma((4,)), dma((4,))],
        0,
        [ANY, VMEM, ANY, ANY] + [VMEM] * 6,
    )
    adjoint, pulled, index_rows, place, starts = call(
        second_kernel,
        [
            cells, shape(6 * CROWS, LANES), shape(CROWS, LANES),
            shape(KLO, WIDE, kind=jnp.int32), shape(8, kind=jnp.int32),
        ],
        [came, cell_diag, adjoint, rest],
        [
            vmem(4 * KLO, WIDE),
            vmem(LANES, SLOTS, kind=BF16),
            vmem(CROWS, SLOTS),
            vmem(8 * CROWS, LANES),
            vmem(4 * CROWS, LANES),
            vmem(BUCKETS, 3 * CY, 2 * BROWS, kind=BF16),
            vmem(BUCKETS, 3 * CY, BROWS),
            diag_tile,
            tile,
            tile,
            dma((3,)),
        ],
        None,
        [VMEM] + [ANY] * 3,
        [VMEM] * 4 + [smem],
    )
    ordered, rest, adjoint_segs, residual_segs = call(
        third_kernel,
        [shape(3 * CROWS, LANES), cells, segs, segs],
        [
            pulled, place, grad_cells, adjoint, cell_diag, cell_off,
            grad_segs, adjoint_segs, seg_diag, chain, lens, seg_slots, push_blocks, pull_blocks,
        ],
        [
            vmem(LANES, SLOTS, kind=BF16),
            vmem(CROWS, SLOTS),
            vmem(6 * CROWS, LANES),
            vmem(ND, 4, ND),
            vmem(ND, 4, ND),
            vmem(ND, KHI, ND),
            vmem(ND, KHI, ND),
            vmem(8 * KLO, WIDE),
            vmem(3 * KLO, WIDE),
            vmem(128, SLOTS, kind=BF16),
            vmem(48, 128),
            vmem(3 * KLO, WIDE),
            off_tile,
            diag_tile,
            tile,
            tile,
            image,
        ]
        + rim_scratch()
        + [dma((4,)), dma((2,)), dma((2,)), dma((2,)), dma((4,)), dma((4,))],
        1,
        [VMEM] * 2 + [ANY] * 4 + [VMEM] * 8,
    )
    residual, adjoint_segs, residual_segs = call(
        fourth_kernel,
        [cells, segs, segs],
        [starts, ordered, rest, index_rows, adjoint_segs, residual_segs],
        [vmem(BUCKETS, 3 * CY, BROWS)],
        None,
        [smem] + [VMEM] * 5,
    )
    return adjoint, adjoint_segs, residual, residual_segs


def solution(mesh):
    in_specs = (
        P(None, None, "gx", "gy"),
        P(None, ("gx", "gy")),
        P(None, None, None, "gx", "gy"),
        P(None, None, None, None, "gx", "gy"),
        P(None, None, ("gx", "gy")),
        P(None, None, None, ("gx", "gy")),
        P(("gx", "gy")),
        P(("gx", "gy"), None),
        P(("gx", "gy")),
        P(("gx", "gy")),
        P(None, None, None, ("gx", "gy")),
    )
    out_specs = (
        P(None, None, "gx", "gy"),
        P(None, ("gx", "gy")),
        P(None, None, "gx", "gy"),
        P(None, ("gx", "gy")),
    )
    return jax.shard_map(shards, mesh=mesh, in_specs=in_specs, out_specs=out_specs, check_vma=False)
```

time: 116 us -> 76.7 us (0.66)
  Pallas kernels: 111 us -> 75.4 us
  local copies, waits for them, and re-layouts: 3.94 us -> 0 us
    pallas_call x1 -> x0, Pallas kernels: 34.2 us -> none  [shards(): pl.pallas_call(second_kernel, out_shape=[cells, shape(ND, 4, ND), shape(C...]
    unnamed x4 -> x0, local copies, waits for them, and re-layouts: 2.6 us -> none
    pallas_call x3 -> x4, Pallas kernels: 77 us -> 75.4 us  [call(): pl.pallas_call(kernel, out_shape=outs, in_specs=in_specs or [VMEM] * len(...]
    reshape x1 -> x0, local copies, waits for them, and re-layouts: 1.34 us -> none  [shards(): lens = seg_len.reshape(32, 1)]
where the time goes in v2:
time: 76.7 us; the launch traced here: 76 us
  Pallas kernels  75.4 us (98%)
    pallas_call x4, Pallas kernels, call(): pl.pallas_call(kernel, out_shape=outs, in_specs=in_specs or [VMEM] * len(...  75.4 us

profile of v2, /device:TPU:1, one launch (start us, length us, event | category | flops | bytes accessed | tf_op | source)
XLA Modules:
  0.0 76.0 jit_solution(4512024572984414236)
XLA Ops:
  0.6 25.6 %first_kernel.1 = (f32[128,2,128]{2,1,0:T(2,128)}, f32[32,256]{1,0:T(8,128)}, f32[288,256]{1,0:T(8,128)}, f32[288,256]{1,0:T(8,128)}, f32[3,32,16,128]{3,2,1,0:T...) custom-call(f32[3,32,16,128]{3,2,1,0:T(8,128)} %grad_cells.3, f32[3,1024]{1,0:T(4,128)} %grad_segs.3, ...), custom_call_target="tpu_custom_call" | custom-call | tf_op jit(solution)/shard_map/first_kernel/pallas_call | solution.py:824
  26.2 11.7 %second_kernel.1 = (f32[3,32,16,128]{3,2,1,0:T(8,128)}, f32[240,256]{1,0:T(8,128)}, f32[40,256]{1,0:T(8,128)}, s32[32,256]{1,0:T(8,128)}, s32[8]{0:T(128)}) custom-call(f32[128,2,128]{2,1,0:T(2,128)} %get-tuple-element.23.came, f32[3,3,32,16,128]{4,3,2,1,0:T(8,128)} %diag.5, f32[3,32,16,128]{3,2,1,0:T(8,128)} %get-tuple-element.24.adjoint, ...), custom_call_target="tpu_custom_call" | custom-call | tf_op jit(solution)/shard_map/second_kernel/pallas_call | solution.py:824
  38.0 33.6 %third_kernel.1 = (f32[120,256]{1,0:T(8,128)}, f32[3,32,16,128]{3,2,1,0:T(8,128)}, f32[3,1024]{1,0:T(4,128)}, f32[3,1024]{1,0:T(4,128)}) custom-call(f32[240,256]{1,0:T(8,128)} %get-tuple-element.28.pulled, s32[32,256]{1,0:T(8,128)} %get-tuple-element.29.place, f32[3,32,16,128]{3,2,1,0:T(8,128)} %grad_cells.3, f32[3,32,16,128]{3,2,1,0:T(8,128)} %get-tuple-element.19.adjoint, ...), custom_call_target="tpu_custom_call" | custom-call | tf_op jit(solution)/shard_map/third_kernel/pallas_call | solution.py:824
  71.6 4.4 %fourth_kernel.1 = (f32[3,32,16,128]{3,2,1,0:T(8,128)}, f32[3,1024]{1,0:T(4,128)}, f32[3,1024]{1,0:T(4,128)}) custom-call(s32[8]{0:T(128)} %get-tuple-element.27.starts, f32[120,256]{1,0:T(8,128)} %get-tuple-element.34.ordered, f32[3,32,16,128]{3,2,1,0:T(8,128)} %get-tuple-element.35.rest, f32[40,256]{1,0:T(8,128)} %get-tuple-element.36.index_rows, ...), custom_call_target="tpu_custom_call" | custom-call | tf_op jit(solution)/shard_map/fourth_kernel/pallas_call | solution.py:824

commit v3 on v2

--- a/solution.py
+++ b/solution.py
@@ -25,6 +25,7 @@
 SLOTS = KLO * WIDE
 BUCKETS = 4
 BROWS = ROWS // BUCKETS
+HALF = CY // 2
 CHUNK = 512
 LANES = 256
 CROWS = 40
@@ -285,41 +286,57 @@
             copy.wait_send()
 
 
-def stencil(adjoint, diag_ref, off_ref, image_ref, halo, column_ref):
-    for c in range(3):
-        image_ref[c] = jnp.zeros((NZ + 2, CX, CY), F32)
+def stencil_sides(adjoint, off_ref, image_ref, halo, column_ref):
     rows = iota((CX, CY), 0)
     lanes = iota((CX, CY), 1)
+
+    def body(z, _):
+        a = adjoint(z)
+        moved = [
+            transposed_rows([[off_ref[e, j, i, z] for i in range(3)] for j in range(3)], a)
+            for e in range(4)
+        ]
+        at = pl.ds(pl.multiple_of(z * CX, CX), CX)
+        for c in range(3):
+            halo.x_out[0, c, pl.ds(z, 1), :] = moved[0][c][CX - 1 : CX]
+            halo.x_out[1, c, pl.ds(z, 1), :] = moved[1][c][0:1]
+            right = pltpu.roll(moved[2][c], 1, 1)
+            left = pltpu.roll(moved[3][c], CY - 1, 1)
+            column_ref[c, at, :] = jnp.where(lanes < HALF, right, left)
+            total = jnp.where(rows == 0, 0.0, pltpu.roll(moved[0][c], 1, 0))
+            total += jnp.where(rows == CX - 1, 0.0, pltpu.roll(moved[1][c], CX - 1, 0))
+            total += jnp.where(lanes == 0, 0.0, right)
+            total += jnp.where(lanes == CY - 1, 0.0, left)
+            image_ref[c, z + 1] = total
+        return 0
+
+    lax.fori_loop(0, NZ, body, 0, unroll=2)
+    for c in range(3):
+        turned = column_ref[c].T
+        halo.y_out[0, c : c + 1, :] = turned[0:1]
+        halo.y_out[1, c : c + 1, :] = turned[CY - 1 : CY]
+    halo.start()
+
+
+def stencil_layers(adjoint, diag_ref, off_ref, image_ref):
+    for c in range(3):
+        image_ref[c, 0] = jnp.zeros((CX, CY), F32)
+        image_ref[c, NZ + 1] = jnp.zeros((CX, CY), F32)
 
     def body(z, _):
         a = adjoint(z)
         own = transposed_rows([[diag_ref[j, i, z] for i in range(3)] for j in range(3)], a)
-        moved = [
+        rising, falling = [
             transposed_rows([[off_ref[e, j, i, z] for i in range(3)] for j in range(3)], a)
-            for e in range(6)
+            for e in (4, 5)
         ]
-        columns = jnp.zeros((CX, CY), F32)
         for c in range(3):
-            total = own[c]
-            halo.x_out[0, c, pl.ds(z, 1), :] = moved[0][c][CX - 1 : CX]
-            halo.x_out[1, c, pl.ds(z, 1), :] = moved[1][c][0:1]
-            total += jnp.where(rows == 0, 0.0, pltpu.roll(moved[0][c], 1, 0))
-            total += jnp.where(rows == CX - 1, 0.0, pltpu.roll(moved[1][c], CX - 1, 0))
-            total += jnp.where(lanes == 0, 0.0, pltpu.roll(moved[2][c], 1, 1))
-            total += jnp.where(lanes == CY - 1, 0.0, pltpu.roll(moved[3][c], CY - 1, 1))
-            columns = jnp.where(lanes == c, pltpu.roll(moved[2][c], 1 + c, 1), columns)
-            columns = jnp.where(lanes == 8 + c, pltpu.roll(moved[3][c], 8 + c, 1), columns)
-            image_ref[c, z + 1] += total
-            image_ref[c, z + 2] += moved[4][c]
-            image_ref[c, z] += moved[5][c]
-        column_ref[pl.ds(pl.multiple_of(z * CX, CX), CX), :] = columns
+            image_ref[c, z + 1] += own[c]
+            image_ref[c, z + 2] += rising[c]
+            image_ref[c, z] += falling[c]
         return 0
 
     lax.fori_loop(0, NZ, body, 0, unroll=2)
-    turned = column_ref[...].T
-    halo.y_out[0] = turned[0:8]
-    halo.y_out[1] = turned[8:16]
-    halo.start()
 
 
 def add_rims(image_ref, halo, column_ref):
@@ -329,24 +346,20 @@
     last_x = jnp.where(gx < GX - 1, 1.0, 0.0)
     first_y = jnp.where(gy > 0, 1.0, 0.0)
     last_y = jnp.where(gy < GY - 1, 1.0, 0.0)
-    came = jnp.concatenate(
-        [halo.y_in[0] * first_y, halo.y_in[1] * last_y, jnp.zeros((CY - 16, ROWS), F32)], axis=0
-    )
-    column_ref[...] = came.T
+    eight = iota((8, ROWS), 0)
+    for c in range(3):
+        top = jnp.where(eight == 0, halo.y_in[0, c : c + 1, :] * first_y, 0.0)
+        bottom = jnp.where(eight == 7, halo.y_in[1, c : c + 1, :] * last_y, 0.0)
+        column_ref[c] = jnp.concatenate([top, jnp.zeros((CY - 16, ROWS), F32), bottom], axis=0).T
     rows = iota((CX, CY), 0)
-    lanes = iota((CX, CY), 1)
 
     def body(z, _):
-        columns = column_ref[pl.ds(pl.multiple_of(z * CX, CX), CX), :]
+        at = pl.ds(pl.multiple_of(z * CX, CX), CX)
         for c in range(3):
             low = halo.x_in[0, c, pl.ds(z, 1), :] * first_x
             high = halo.x_in[1, c, pl.ds(z, 1), :] * last_x
             total = jnp.where(rows == 0, low, 0.0) + jnp.where(rows == CX - 1, high, 0.0)
-            left = columns if c == 0 else pltpu.roll(columns, CY - c, 1)
-            total += jnp.where(lanes == 0, left, 0.0)
-            right = pltpu.roll(columns, CY - 1 - 8 - c, 1)
-            total += jnp.where(lanes == CY - 1, right, 0.0)
-            image_ref[c, z + 1] += total
+            image_ref[c, z + 1] += total + column_ref[c, at, :]
         return 0
 
     lax.fori_loop(0, NZ, body, 0, unroll=2)
@@ -393,11 +406,11 @@
 
 def first_kernel(
     grad_cells, grad_segs, diag, off, seg_diag, seg_len, device, local, seg, blocks,
-    came, seg_slots, push_blocks, pull_blocks, adjoint_out, rest_out, adjoint_segs_out,
-    column_hot, row_hot, work, total, slots, lane_hot, table, push, message,
-    off_here, diag_here, grad_here, image,
+    came, seg_slots_out, push_out, pull_out, adjoint_out, rest_out, adjoint_segs_out,
+    column_hot, row_hot, work, total, slots, pull_blocks, lane_hot, table, push, message,
+    off_here, diag_here, grad_here, adjoint, image,
     x_out, x_in, y_out, y_in, column,
-    load_sem, send_sem, recv_sem, own_sem, halo_send, halo_recv,
+    load_sem, store_sem, send_sem, recv_sem, own_sem, halo_send, halo_recv,
 ):
     loads = [
         pltpu.make_async_copy(a, b, load_sem.at[n])
@@ -426,16 +439,25 @@
     ]
     for c in range(3):
         adjoint_segs_out[c : c + 1, :] = adjoint_segs[c]
-    seg_slots[...] = slots[KLO : 2 * KLO, :]
-    push_blocks[...] = slots[2 * KLO :, :]
+    seg_slots = slots.at[pl.ds(KLO, KLO)]
+    push_blocks = slots.at[pl.ds(2 * KLO, 9 * KLO)]
+    stores = [
+        pltpu.make_async_copy(a, b, store_sem.at[n])
+        for n, (a, b) in enumerate(
+            [
+                (seg_slots, seg_slots_out), (push_blocks, push_out),
+                (adjoint, adjoint_out), (pull_blocks, pull_out), (grad_here, rest_out),
+            ]
+        )
+    ]
+    stores[0].start()
+    stores[1].start()
     lane_hots(seg_slots, lane_hot)
     seg_gather(adjoint_segs, seg_slots, lane_hot, table, push)
     terms = slot_terms(push_blocks, push, 0)
     packed = jnp.concatenate([slots[0:KLO, :]] + terms, axis=0)
     for h in range(KHI):
         message[:, h, :] = packed[:, ND * h : ND * (h + 1)].T
-    greeted()
-    exchange.start()
     loads[0].wait()
     loads[1].wait()
 
@@ -444,21 +466,29 @@
             [[diag_here[i, j, z] for j in range(3)] for i in range(3)], cells_at(grad_here, z)
         )
         for c in range(3):
-            adjoint_out[c, z] = a[c]
+            adjoint[c, z] = a[c]
         return 0
 
     lax.fori_loop(0, NZ, begin, 0, unroll=2)
+    stores[2].start()
     loads[2].wait()
-    stencil(lambda z: cells_at(adjoint_out, z), diag_here, off_here, image, halo, column)
+    greeted()
+    stencil_sides(lambda z: cells_at(adjoint, z), off_here, image, halo, column)
+    exchange.start()
+    stencil_layers(lambda z: cells_at(adjoint, z), diag_here, off_here, image)
     place_rows(
         lambda q, at: blocks[q // 3, q % 3, 1:2, at],
         9, column_hot, row_hot, work, total, pull_blocks,
     )
+    stores[3].start()
     halo.wait_recv()
     add_rims(image, halo, column)
     for c in range(3):
-        rest_out[c] = grad_here[c] - image[c, 1 : NZ + 1]
+        grad_here[c] = grad_here[c] - image[c, 1 : NZ + 1]
+    stores[4].start()
     exchange.wait_recv()
+    for store in stores:
+        store.wait()
     exchange.wait_send()
     halo.wait_send()
 
@@ -549,30 +579,35 @@
 def turn_cells(cells, turned_ref):
     for c in range(3):
         for b in range(BUCKETS):
-            block = cells(c, b).T
-            high, low = halves(block)
-            at = slice(c * CY, (c + 1) * CY)
-            turned_ref[b, at, 0:BROWS] = high.astype(BF16)
-            turned_ref[b, at, BROWS : 2 * BROWS] = low.astype(BF16)
-
-
-def two_rows(ref, start, j):
-    return jnp.concatenate([ref[pl.ds(start + 2 * j + n, 1), :] for n in range(2)], axis=1)
+            for p, part in enumerate(halves(cells(c, b).T)):
+                at = (3 * p + c) * HALF
+                turned_ref[b, at : at + HALF, 0:BROWS] = part[:HALF].astype(BF16)
+                turned_ref[b, at : at + HALF, BROWS : 2 * BROWS] = part[HALF:].astype(BF16)
+
+
+def chunk_row(ref, start, j):
+    rows = CHUNK // LANES
+    if rows == 1:
+        return ref[pl.ds(start + j, 1), :]
+    return jnp.concatenate([ref[pl.ds(start + rows * j + n, 1), :] for n in range(rows)], axis=1)
 
 
 def chunk_hots(index_ref, j, b):
-    index = two_rows(index_ref, 0, j).astype(jnp.int32) - 1
-    row = one_hot(BROWS, (index >> 7) - BROWS * b, BF16)
-    lane = one_hot(CY, index & 127, F32)
+    index = chunk_row(index_ref, 0, j).astype(jnp.int32) - 1
+    row = (index >> 7) - BROWS * b + ((index >> 6) & 1) * BROWS
+    row = one_hot(2 * BROWS, jnp.where(index >= 0, row, -1), BF16)
+    lane = one_hot(HALF, index & (HALF - 1), F32)
     return row, lane
 
 
 def gather_chunk(turned, row, lane, out_ref, start, j):
-    found = jnp.dot(turned, jnp.concatenate([row, row], axis=0), preferred_element_type=F32)
-    for c in range(3):
-        value = jnp.sum(found[c * CY : (c + 1) * CY] * lane, axis=0, keepdims=True)
-        for n in range(2):
-            out_ref[pl.ds(start + c * CROWS + 2 * j + n, 1), :] = value[
+    found = jnp.dot(turned, row, preferred_element_type=F32)
+    found = found[: 3 * HALF] + found[3 * HALF :]
+    for c in range(3):
+        value = jnp.sum(found[c * HALF : (c + 1) * HALF] * lane, axis=0, keepdims=True)
+        rows = CHUNK // LANES
+        for n in range(rows):
+            out_ref[pl.ds(start + c * CROWS + rows * j + n, 1), :] = value[
                 :, LANES * n : LANES * (n + 1)
             ]
 
@@ -580,13 +615,13 @@
 def scatter_chunk(values_ref, start, j, row, lane, total_ref, b):
     high, low = [], []
     for c in range(3):
-        one, two = halves(two_rows(values_ref, start + c * CROWS, j))
+        one, two = halves(chunk_row(values_ref, start + c * CROWS, j))
         high.append(lane * one)
         low.append(lane * two)
     part = lax.dot_general(
         jnp.concatenate(high + low, axis=0).astype(BF16), row, NT, preferred_element_type=F32
     )
-    total_ref[b] += part[: 3 * CY] + part[3 * CY :]
+    total_ref[b] += part[: 3 * HALF] + part[3 * HALF :]
 
 
 def each_chunk(starts, act):
@@ -604,7 +639,9 @@
 
 
 def scattered_cells(total_ref, b, c):
-    return total_ref[b, c * CY : (c + 1) * CY, :].T.reshape(NZ // BUCKETS, CX, CY)
+    part = total_ref[b, c * HALF : (c + 1) * HALF, :]
+    whole = jnp.concatenate([part[:, :BROWS], part[:, BROWS:]], axis=0)
+    return whole.T.reshape(NZ // BUCKETS, CX, CY)
 
 
 def unpack(came, rows_ref, comps):
@@ -616,7 +653,7 @@
     came, diag, adjoint, rest,
     adjoint_out, pulled, index_out, place, starts_out,
     rows, lane_hot, chunk_hot, total, ordered, turned, scattered,
-    diag_here, adjoint_here, rest_here, load_sem,
+    diag_here, adjoint_here, rest_here, load_sem, store_sem,
 ):
     loads = [
         pltpu.make_async_copy(a, b, load_sem.at[n])
@@ -659,12 +696,14 @@
             [[diag_here[i, j, z] for j in range(3)] for i in range(3)], cells_at(rest_here, z)
         )
         for c in range(3):
-            adjoint_out[c, z] = adjoint_here[c, z] + step[c]
+            adjoint_here[c, z] += step[c]
         return 0
 
     lax.fori_loop(0, NZ, update, 0, unroll=2)
+    store = pltpu.make_async_copy(adjoint_here, adjoint_out, store_sem)
+    store.start()
     turn_cells(
-        lambda c, b: adjoint_out[c, 8 * b : 8 * b + 8].reshape(BROWS, CY),
+        lambda c, b: adjoint_here[c, 8 * b : 8 * b + 8].reshape(BROWS, CY),
         turned,
     )
 
@@ -676,6 +715,7 @@
     index_out[...] = ordered[0:CROWS, :]
     for b in range(BUCKETS + 1):
         starts_out[b] = starts[b]
+    store.wait()
 
 
 def seg_image(adjoint, diag, chain, scattered):
@@ -700,10 +740,10 @@
     pulled, place, grad_cells, adjoint, diag, off,
     grad_segs, adjoint_segs, seg_diag, seg_chain, seg_len, seg_slots, push_blocks, pull_blocks,
     ordered, rest_out, adjoint_segs_out, residual_segs_out,
-    place_lane, place_chunk, total, message, pulls_in, push_message, came,
+    place_lane, place_chunk, total, message, pulls_in, late_message, late_in, push_message, came,
     pulls, terms, lane_hot, table, push, off_here, diag_here, grad_here, adjoint_here, image,
     x_out, x_in, y_out, y_in, column,
-    load_sem, send_sem, recv_sem, own_sem, halo_send, halo_recv,
+    load_sem, store_sem, send_sem, recv_sem, own_sem, halo_send, halo_recv,
 ):
     greet()
     loads = [
@@ -721,30 +761,36 @@
     push_exchange = Exchange(
         push_message, came, send_sem.at[1], recv_sem.at[1], own_sem.at[1]
     )
+    late_exchange = Exchange(
+        late_message, late_in, send_sem.at[2], recv_sem.at[2], own_sem.at[2]
+    )
     halo = Halo(x_out, x_in, y_out, y_in, halo_send, halo_recv)
     place_hots(place, place_lane, place_chunk)
     pulls[...] = jnp.zeros_like(pulls)
     from_places(
-        pulled, 6, place_lane, place_chunk, pulls,
-        [q * KLO + (q // 3) * KLO for q in range(6)],
+        pulled.at[pl.ds(0, 3 * CROWS)], 3, place_lane, place_chunk, pulls, [0, KLO, 2 * KLO]
     )
     for h in range(KHI):
-        for n in range(2):
-            message[:, 2 * h + n, :] = pulls[ND * n : ND * (n + 1), ND * h : ND * (h + 1)].T
+        message[:, h, :] = pulls[0:ND, ND * h : ND * (h + 1)].T
+    lane_hots(seg_slots, lane_hot)
     greeted()
     pull_exchange.start()
+    from_places(
+        pulled.at[pl.ds(3 * CROWS, 3 * CROWS)], 3, place_lane, place_chunk, pulls,
+        [ND, ND + KLO, ND + 2 * KLO],
+    )
+    for h in range(KHI):
+        late_message[:, h, :] = pulls[ND : 2 * ND, ND * h : ND * (h + 1)].T
+    late_exchange.start()
     for load in loads[:3]:
         load.wait()
-    stencil(lambda z: cells_at(adjoint_here, z), diag_here, off_here, image, halo, column)
-    lane_hots(seg_slots, lane_hot)
+    stencil_sides(lambda z: cells_at(adjoint_here, z), off_here, image, halo, column)
     active = active_row(seg_len)
     grad = seg_rows(grad_segs)
     matrix = seg_matrix(seg_diag)
     before = seg_rows(adjoint_segs)
     pull_exchange.wait_recv()
-    for h in range(KHI):
-        for n in range(2):
-            pulls[ND * n : ND * (n + 1), ND * h : ND * (h + 1)] = pulls_in[:, 2 * h + n, :].T
+    unpack(pulls_in, pulls, 3)
     for c, term in enumerate(slot_terms(pull_blocks, pulls, 0)):
         terms[c * KLO : (c + 1) * KLO, :] = term
     scattered = seg_scatter(terms, seg_slots, lane_hot, table)
@@ -760,7 +806,10 @@
     for h in range(KHI):
         push_message[:, h, :] = packed[:, ND * h : ND * (h + 1)].T
     push_exchange.start()
-    for c, term in enumerate(slot_terms(pull_blocks, pulls, ND)):
+    stencil_layers(lambda z: cells_at(adjoint_here, z), diag_here, off_here, image)
+    late_exchange.wait_recv()
+    unpack(late_in, pulls, 3)
+    for c, term in enumerate(slot_terms(pull_blocks, pulls, 0)):
         terms[c * KLO : (c + 1) * KLO, :] = term
     scattered = seg_scatter(terms, seg_slots, lane_hot, table)
     seen = seg_image(after, seg_diag, seg_chain, scattered)
@@ -770,10 +819,14 @@
     add_rims(image, halo, column)
     loads[3].wait()
     for c in range(3):
-        rest_out[c] = grad_here[c] - image[c, 1 : NZ + 1]
+        grad_here[c] = grad_here[c] - image[c, 1 : NZ + 1]
+    store = pltpu.make_async_copy(grad_here, rest_out, store_sem)
+    store.start()
     push_exchange.wait_recv()
     unpack(came, pulls, 3)
     to_places(pulls, 3, place_lane, place_chunk, total, ordered)
+    store.wait()
+    late_exchange.wait_send()
     pull_exchange.wait_send()
     push_exchange.wait_send()
     halo.wait_send()
@@ -811,9 +864,9 @@
     return [
         vmem(2, 3, NZ, CY),
         vmem(2, 3, NZ, CY),
-        vmem(2, 8, ROWS),
-        vmem(2, 8, ROWS),
-        vmem(ROWS, CY),
+        vmem(2, 3, ROWS),
+        vmem(2, 3, ROWS),
+        vmem(3, ROWS, CY),
     ]
 
 
@@ -863,6 +916,7 @@
             vmem(22 * KLO, 512, kind=BF16),
             vmem(22 * KLO, WIDE),
             vmem(11 * KLO, WIDE),
+            vmem(9 * KLO, WIDE),
             vmem(128, SLOTS, kind=BF16),
             vmem(48, 128),
             vmem(3 * KLO, WIDE),
@@ -870,12 +924,14 @@
             off_tile,
             diag_tile,
             tile,
+            tile,
             image,
         ]
         + rim_scratch()
-        + [dma((3,)), dma, dma, dma, dma((4,)), dma((4,))],
+        + [dma((3,)), dma((5,)), dma, dma, dma, dma((4,)), dma((4,))],
         0,
         [ANY, VMEM, ANY, ANY] + [VMEM] * 6,
+        [VMEM] + [ANY] * 5 + [VMEM],
     )
     adjoint, pulled, index_rows, place, starts = call(
         second_kernel,
@@ -890,16 +946,17 @@
             vmem(CROWS, SLOTS),
             vmem(8 * CROWS, LANES),
             vmem(4 * CROWS, LANES),
-            vmem(BUCKETS, 3 * CY, 2 * BROWS, kind=BF16),
-            vmem(BUCKETS, 3 * CY, BROWS),
+            vmem(BUCKETS, 6 * HALF, 2 * BROWS, kind=BF16),
+            vmem(BUCKETS, 3 * HALF, 2 * BROWS),
             diag_tile,
             tile,
             tile,
             dma((3,)),
+            dma,
         ],
         None,
         [VMEM] + [ANY] * 3,
-        [VMEM] * 4 + [smem],
+        [ANY] + [VMEM] * 3 + [smem],
     )
     ordered, rest, adjoint_segs, residual_segs = call(
         third_kernel,
@@ -912,8 +969,10 @@
             vmem(LANES, SLOTS, kind=BF16),
             vmem(CROWS, SLOTS),
             vmem(6 * CROWS, LANES),
-            vmem(ND, 4, ND),
-            vmem(ND, 4, ND),
+            vmem(ND, KHI, ND),
+            vmem(ND, KHI, ND),
+            vmem(ND, KHI, ND),
+            vmem(ND, KHI, ND),
             vmem(ND, KHI, ND),
             vmem(ND, KHI, ND),
             vmem(8 * KLO, WIDE),
@@ -928,15 +987,16 @@
             image,
         ]
         + rim_scratch()
-        + [dma((4,)), dma((2,)), dma((2,)), dma((2,)), dma((4,)), dma((4,))],
+        + [dma((4,)), dma, dma((3,)), dma((3,)), dma((3,)), dma((4,)), dma((4,))],
         1,
         [VMEM] * 2 + [ANY] * 4 + [VMEM] * 8,
+        [VMEM, ANY, VMEM, VMEM],
     )
     residual, adjoint_segs, residual_segs = call(
         fourth_kernel,
         [cells, segs, segs],
         [starts, ordered, rest, index_rows, adjoint_segs, residual_segs],
-        [vmem(BUCKETS, 3 * CY, BROWS)],
+        [vmem(BUCKETS, 3 * HALF, 2 * BROWS)],
         None,
         [smem] + [VMEM] * 5,
     )

time: 76.7 us -> 72.3 us (0.943)
  Pallas kernels: 75.4 us -> 71.2 us
    pallas_call x4, Pallas kernels: 75.4 us -> 71.2 us  [call(): pl.pallas_call(kernel, out_shape=outs, in_specs=in_specs or [VMEM] * len(...]
where the time goes in v3:
time: 72.3 us; the launch traced here: 71.8 us
  Pallas kernels  71.2 us (98%)
    pallas_call x4, Pallas kernels, call(): pl.pallas_call(kernel, out_shape=outs, in_specs=in_specs or [VMEM] * len(...  71.2 us

profile of v3, /device:TPU:1, one launch (start us, length us, event | category | flops | bytes accessed | tf_op | source)
XLA Modules:
  0.0 71.8 jit_solution(3849522582913567888)
XLA Ops:
  0.6 24.7 %first_kernel.1 = (f32[128,2,128]{2,1,0:T(2,128)}, f32[32,256]{1,0:T(8,128)}, f32[288,256]{1,0:T(8,128)}, f32[288,256]{1,0:T(8,128)}, f32[3,32,16,128]{3,2,1,0:T...) custom-call(f32[3,32,16,128]{3,2,1,0:T(8,128)} %grad_cells.3, f32[3,1024]{1,0:T(4,128)} %grad_segs.3, ...), custom_call_target="tpu_custom_call" | custom-call | tf_op jit(solution)/shard_map/first_kernel/pallas_call | solution.py:877
  25.3 10.5 %second_kernel.1 = (f32[3,32,16,128]{3,2,1,0:T(8,128)}, f32[240,256]{1,0:T(8,128)}, f32[40,256]{1,0:T(8,128)}, s32[32,256]{1,0:T(8,128)}, s32[8]{0:T(128)}) custom-call(f32[128,2,128]{2,1,0:T(2,128)} %get-tuple-element.23.came, f32[3,3,32,16,128]{4,3,2,1,0:T(8,128)} %diag.5, f32[3,32,16,128]{3,2,1,0:T(8,128)} %get-tuple-element.24.adjoint, ...), custom_call_target="tpu_custom_call" | custom-call | tf_op jit(solution)/shard_map/second_kernel/pallas_call | solution.py:877
  35.8 32.4 %third_kernel.1 = (f32[120,256]{1,0:T(8,128)}, f32[3,32,16,128]{3,2,1,0:T(8,128)}, f32[3,1024]{1,0:T(4,128)}, f32[3,1024]{1,0:T(4,128)}) custom-call(f32[240,256]{1,0:T(8,128)} %get-tuple-element.28.pulled, s32[32,256]{1,0:T(8,128)} %get-tuple-element.29.place, f32[3,32,16,128]{3,2,1,0:T(8,128)} %grad_cells.3, f32[3,32,16,128]{3,2,1,0:T(8,128)} %get-tuple-element.19.adjoint, ...), custom_call_target="tpu_custom_call" | custom-call | tf_op jit(solution)/shard_map/third_kernel/pallas_call | solution.py:877
  68.2 3.6 %fourth_kernel.1 = (f32[3,32,16,128]{3,2,1,0:T(8,128)}, f32[3,1024]{1,0:T(4,128)}, f32[3,1024]{1,0:T(4,128)}) custom-call(s32[8]{0:T(128)} %get-tuple-element.27.starts, f32[120,256]{1,0:T(8,128)} %get-tuple-element.34.ordered, f32[3,32,16,128]{3,2,1,0:T(8,128)} %get-tuple-element.35.rest, f32[40,256]{1,0:T(8,128)} %get-tuple-element.36.index_rows, ...), custom_call_target="tpu_custom_call" | custom-call | tf_op jit(solution)/shard_map/fourth_kernel/pallas_call | solution.py:877

commit v4 on v3

--- a/solution.py
+++ b/solution.py
@@ -184,14 +184,19 @@
 def everyone(act):
     gx = lax.axis_index("gx")
     gy = lax.axis_index("gy")
-    me = gx * GY + gy
+    columns = [lax.rem(gy + j, GY) for j in range(GY)]
+
+    def visit(row, distances):
+        for j in distances:
+            act(row * GY + columns[j], (row, columns[j]))
+
+    visit(gx, range(1, GY))
 
     def body(i, _):
-        other = lax.rem(me + i, ND)
-        act(other, (other // GY, lax.rem(other, GY)))
+        visit(lax.rem(gx + i, GX), range(GY))
         return 0
 
-    lax.fori_loop(1, ND, body, 0)
+    lax.fori_loop(1, GX, body, 0)
 
 
 def greet():
@@ -526,28 +531,30 @@
     return starts
 
 
-def place_hots(place_ref, lane_ref, chunk_ref):
+def built_hots(place_ref, k):
+    place = four_rows(place_ref, 0, k)
+    return one_hot(LANES, place & (LANES - 1), BF16), one_hot(CROWS, place >> 8, F32)
+
+
+def kept_hots(place_ref, lane_ref, chunk_ref, k):
+    lane, chunk = built_hots(place_ref, k)
+    lane_ref[:, four_lanes(k)] = lane
+    chunk_ref[:, four_lanes(k)] = chunk
+    return lane, chunk
+
+
+def to_places(rows_ref, count, hots, total_ref, out_ref):
+    size = count * CROWS
+
     def body(k, _):
-        place = four_rows(place_ref, 0, k)
-        lane_ref[:, four_lanes(k)] = one_hot(LANES, place & (LANES - 1), BF16)
-        chunk_ref[:, four_lanes(k)] = one_hot(CROWS, place >> 8, F32)
-        return 0
-
-    lax.fori_loop(0, KLO // 4, body, 0)
-
-
-def to_places(rows_ref, count, lane_ref, chunk_ref, total_ref, out_ref):
-    size = count * CROWS
-
-    def body(k, _):
-        chunk = chunk_ref[:, four_lanes(k)]
+        lane, chunk = hots(k)
         left = [[], []]
         for q in range(count):
             for p, part in enumerate(halves(four_rows(rows_ref, q * KLO, k))):
                 left[p].append(chunk * part)
         total_ref[0 : 2 * size, :] += lax.dot_general(
             jnp.concatenate(left[0] + left[1], axis=0).astype(BF16),
-            lane_ref[:, four_lanes(k)],
+            lane,
             NT,
             preferred_element_type=F32,
         )
@@ -558,13 +565,13 @@
     out_ref[...] = total_ref[0:size, :] + total_ref[size : 2 * size, :]
 
 
-def from_places(rows_ref, count, lane_ref, chunk_ref, out_ref, starts):
+def from_places(rows_ref, count, hots, out_ref, starts):
     size = count * CROWS
     both = jnp.concatenate(halves(rows_ref[...]), axis=0).astype(BF16)
 
     def body(k, _):
-        chunk = chunk_ref[:, four_lanes(k)]
-        found = jnp.dot(both, lane_ref[:, four_lanes(k)], preferred_element_type=F32)
+        lane, chunk = hots(k)
+        found = jnp.dot(both, lane, preferred_element_type=F32)
         for q in range(count):
             at = q * CROWS
             value = found[at : at + CROWS] + found[size + at : size + at + CROWS]
@@ -652,7 +659,7 @@
 def second_kernel(
     came, diag, adjoint, rest,
     adjoint_out, pulled, index_out, place, starts_out,
-    rows, lane_hot, chunk_hot, total, ordered, turned, scattered,
+    rows, total, ordered, turned, scattered,
     diag_here, adjoint_here, rest_here, load_sem, store_sem,
 ):
     loads = [
@@ -667,8 +674,7 @@
     index = rows[0:KLO, :].astype(jnp.int32)
     starts = bucket_starts(index)
     place_slots(index, place, starts)
-    place_hots(place, lane_hot, chunk_hot)
-    to_places(rows, 4, lane_hot, chunk_hot, total, ordered)
+    to_places(rows, 4, lambda k: built_hots(place, k), total, ordered)
     loads[0].wait()
     turn_cells(
         lambda c, b: adjoint_here[c, 8 * b : 8 * b + 8].reshape(BROWS, CY),
@@ -765,18 +771,22 @@
         late_message, late_in, send_sem.at[2], recv_sem.at[2], own_sem.at[2]
     )
     halo = Halo(x_out, x_in, y_out, y_in, halo_send, halo_recv)
-    place_hots(place, place_lane, place_chunk)
     pulls[...] = jnp.zeros_like(pulls)
     from_places(
-        pulled.at[pl.ds(0, 3 * CROWS)], 3, place_lane, place_chunk, pulls, [0, KLO, 2 * KLO]
-    )
+        pulled.at[pl.ds(0, 3 * CROWS)], 3,
+        lambda k: kept_hots(place, place_lane, place_chunk, k), pulls, [0, KLO, 2 * KLO],
+    )
+
+    def hots(k):
+        return place_lane[:, four_lanes(k)], place_chunk[:, four_lanes(k)]
+
     for h in range(KHI):
         message[:, h, :] = pulls[0:ND, ND * h : ND * (h + 1)].T
     lane_hots(seg_slots, lane_hot)
     greeted()
     pull_exchange.start()
     from_places(
-        pulled.at[pl.ds(3 * CROWS, 3 * CROWS)], 3, place_lane, place_chunk, pulls,
+        pulled.at[pl.ds(3 * CROWS, 3 * CROWS)], 3, hots, pulls,
         [ND, ND + KLO, ND + 2 * KLO],
     )
     for h in range(KHI):
@@ -824,7 +834,7 @@
     store.start()
     push_exchange.wait_recv()
     unpack(came, pulls, 3)
-    to_places(pulls, 3, place_lane, place_chunk, total, ordered)
+    to_places(pulls, 3, hots, total, ordered)
     store.wait()
     late_exchange.wait_send()
     pull_exchange.wait_send()
@@ -942,8 +952,6 @@
         [came, cell_diag, adjoint, rest],
         [
             vmem(4 * KLO, WIDE),
-            vmem(LANES, SLOTS, kind=BF16),
-            vmem(CROWS, SLOTS),
             vmem(8 * CROWS, LANES),
             vmem(4 * CROWS, LANES),
             vmem(BUCKETS, 6 * HALF, 2 * BROWS, kind=BF16),

time: 72.3 us -> 65.1 us (0.900)
  Pallas kernels: 71.2 us -> 64.3 us
    pallas_call x4, Pallas kernels: 71.2 us -> 64.3 us  [call(): pl.pallas_call(kernel, out_shape=outs, in_specs=in_specs or [VMEM] * len(...]
where the time goes in v4:
time: 65.1 us; the launch traced here: 64.9 us
  Pallas kernels  64.3 us (99%)
  between operations  0.66 us (1%)
    pallas_call x4, Pallas kernels, call(): pl.pallas_call(kernel, out_shape=outs, in_specs=in_specs or [VMEM] * len(...  64.3 us

profile of v4, /device:TPU:1, one launch (start us, length us, event | category | flops | bytes accessed | tf_op | source)
XLA Modules:
  0.0 64.9 jit_solution(13468217265209363230)
XLA Ops:
  0.6 22.9 %first_kernel.1 = (f32[128,2,128]{2,1,0:T(2,128)}, f32[32,256]{1,0:T(8,128)}, f32[288,256]{1,0:T(8,128)}, f32[288,256]{1,0:T(8,128)}, f32[3,32,16,128]{3,2,1,0:T...) custom-call(f32[3,32,16,128]{3,2,1,0:T(8,128)} %grad_cells.3, f32[3,1024]{1,0:T(4,128)} %grad_segs.3, ...), custom_call_target="tpu_custom_call" | custom-call | tf_op jit(solution)/shard_map/first_kernel/pallas_call | solution.py:887
  23.6 9.4 %second_kernel.1 = (f32[3,32,16,128]{3,2,1,0:T(8,128)}, f32[240,256]{1,0:T(8,128)}, f32[40,256]{1,0:T(8,128)}, s32[32,256]{1,0:T(8,128)}, s32[8]{0:T(128)}) custom-call(f32[128,2,128]{2,1,0:T(2,128)} %get-tuple-element.23.came, f32[3,3,32,16,128]{4,3,2,1,0:T(8,128)} %diag.5, f32[3,32,16,128]{3,2,1,0:T(8,128)} %get-tuple-element.24.adjoint, ...), custom_call_target="tpu_custom_call" | custom-call | tf_op jit(solution)/shard_map/second_kernel/pallas_call | solution.py:887
  32.9 28.4 %third_kernel.1 = (f32[120,256]{1,0:T(8,128)}, f32[3,32,16,128]{3,2,1,0:T(8,128)}, f32[3,1024]{1,0:T(4,128)}, f32[3,1024]{1,0:T(4,128)}) custom-call(f32[240,256]{1,0:T(8,128)} %get-tuple-element.28.pulled, s32[32,256]{1,0:T(8,128)} %get-tuple-element.29.place, f32[3,32,16,128]{3,2,1,0:T(8,128)} %grad_cells.3, f32[3,32,16,128]{3,2,1,0:T(8,128)} %get-tuple-element.19.adjoint, ...), custom_call_target="tpu_custom_call" | custom-call | tf_op jit(solution)/shard_map/third_kernel/pallas_call | solution.py:887
  61.3 3.6 %fourth_kernel.1 = (f32[3,32,16,128]{3,2,1,0:T(8,128)}, f32[3,1024]{1,0:T(4,128)}, f32[3,1024]{1,0:T(4,128)}) custom-call(s32[8]{0:T(128)} %get-tuple-element.27.starts, f32[120,256]{1,0:T(8,128)} %get-tuple-element.34.ordered, f32[3,32,16,128]{3,2,1,0:T(8,128)} %get-tuple-element.35.rest, f32[40,256]{1,0:T(8,128)} %get-tuple-element.36.index_rows, ...), custom_call_target="tpu_custom_call" | custom-call | tf_op jit(solution)/shard_map/fourth_kernel/pallas_call | solution.py:887

commit v5 on v4

--- a/solution.py
+++ b/solution.py
@@ -524,11 +524,13 @@
 def bucket_starts(index):
     row = (index - 1) >> 7
     starts = [jnp.int32(0)]
+    most = jnp.int32(0)
     for b in range(BUCKETS):
         held = ((index > 0) & ((row // BROWS) == b)).astype(jnp.int32)
         count = jnp.sum(held)
         starts.append(starts[-1] + (count + CHUNK - 1) // CHUNK)
-    return starts
+        most = jnp.maximum(most, (count + LANES - 1) // LANES)
+    return starts + [most]
 
 
 def built_hots(place_ref, k):
@@ -592,37 +594,33 @@
                 turned_ref[b, at : at + HALF, BROWS : 2 * BROWS] = part[HALF:].astype(BF16)
 
 
-def chunk_row(ref, start, j):
-    rows = CHUNK // LANES
-    if rows == 1:
-        return ref[pl.ds(start + j, 1), :]
-    return jnp.concatenate([ref[pl.ds(start + rows * j + n, 1), :] for n in range(rows)], axis=1)
-
-
-def chunk_hots(index_ref, j, b):
-    index = chunk_row(index_ref, 0, j).astype(jnp.int32) - 1
+def chunk_row(ref, row, rows):
+    return jnp.concatenate([ref[pl.ds(row + n, 1), :] for n in range(rows)], axis=1)
+
+
+def chunk_hots(index_ref, j, rows, b):
+    index = chunk_row(index_ref, j, rows).astype(jnp.int32) - 1
     row = (index >> 7) - BROWS * b + ((index >> 6) & 1) * BROWS
     row = one_hot(2 * BROWS, jnp.where(index >= 0, row, -1), BF16)
     lane = one_hot(HALF, index & (HALF - 1), F32)
     return row, lane
 
 
-def gather_chunk(turned, row, lane, out_ref, start, j):
+def gather_chunk(turned, row, lane, out_ref, start, j, rows):
     found = jnp.dot(turned, row, preferred_element_type=F32)
     found = found[: 3 * HALF] + found[3 * HALF :]
     for c in range(3):
         value = jnp.sum(found[c * HALF : (c + 1) * HALF] * lane, axis=0, keepdims=True)
-        rows = CHUNK // LANES
         for n in range(rows):
-            out_ref[pl.ds(start + c * CROWS + rows * j + n, 1), :] = value[
+            out_ref[pl.ds(start + c * CROWS + j + n, 1), :] = value[
                 :, LANES * n : LANES * (n + 1)
             ]
 
 
-def scatter_chunk(values_ref, start, j, row, lane, total_ref, b):
+def scatter_chunk(values_ref, start, j, rows, row, lane, total_ref, b):
     high, low = [], []
     for c in range(3):
-        one, two = halves(chunk_row(values_ref, start + c * CROWS, j))
+        one, two = halves(chunk_row(values_ref, start + c * CROWS + j, rows))
         high.append(lane * one)
         low.append(lane * two)
     part = lax.dot_general(
@@ -633,16 +631,18 @@
 
 def each_chunk(starts, act):
     counts = [starts[b + 1] - starts[b] for b in range(BUCKETS)]
-    steps = counts[0]
-    for count in counts[1:]:
-        steps = jnp.maximum(steps, count)
-
-    def body(t, _):
-        for b in range(BUCKETS):
-            act(b, jnp.where(t < counts[b], starts[b] + t, SPARE))
-        return 0
-
-    lax.fori_loop(0, steps, body, 0)
+    steps = starts[BUCKETS + 1] // 2
+
+    def step(rows):
+        def body(t, _):
+            for b in range(BUCKETS):
+                act(b, 2 * jnp.where(t < counts[b], starts[b] + t, SPARE), rows)
+            return 0
+
+        return body
+
+    lax.fori_loop(0, steps, step(2), 0)
+    lax.fori_loop(steps, starts[BUCKETS + 1] - steps, step(1), 0)
 
 
 def scattered_cells(total_ref, b, c):
@@ -684,10 +684,10 @@
     pulled[...] = jnp.zeros_like(pulled)
     index_rows = ordered.at[pl.ds(0, CROWS)]
 
-    def first(b, j):
-        row, lane = chunk_hots(index_rows, j, b)
-        gather_chunk(turned[b], row, lane, pulled, 0, j)
-        scatter_chunk(ordered, CROWS, j, row, lane, scattered, b)
+    def first(b, j, n):
+        row, lane = chunk_hots(index_rows, j, n, b)
+        gather_chunk(turned[b], row, lane, pulled, 0, j, n)
+        scatter_chunk(ordered, CROWS, j, n, row, lane, scattered, b)
 
     each_chunk(starts, first)
     loads[1].wait()
@@ -713,13 +713,13 @@
         turned,
     )
 
-    def second(b, j):
-        row, lane = chunk_hots(index_rows, j, b)
-        gather_chunk(turned[b], row, lane, pulled, 3 * CROWS, j)
+    def second(b, j, n):
+        row, lane = chunk_hots(index_rows, j, n, b)
+        gather_chunk(turned[b], row, lane, pulled, 3 * CROWS, j, n)
 
     each_chunk(starts, second)
     index_out[...] = ordered[0:CROWS, :]
-    for b in range(BUCKETS + 1):
+    for b in range(BUCKETS + 2):
         starts_out[b] = starts[b]
     store.wait()
 
@@ -851,11 +851,11 @@
     residual_segs_out[...] = residual_segs[...]
     scattered[...] = jnp.zeros_like(scattered)
 
-    def act(b, j):
-        row, lane = chunk_hots(index_rows, j, b)
-        scatter_chunk(ordered, 0, j, row, lane, scattered, b)
-
-    each_chunk([starts[b] for b in range(BUCKETS + 1)], act)
+    def act(b, j, n):
+        row, lane = chunk_hots(index_rows, j, n, b)
+        scatter_chunk(ordered, 0, j, n, row, lane, scattered, b)
+
+    each_chunk([starts[b] for b in range(BUCKETS + 2)], act)
     for b in range(BUCKETS):
         for c in range(3):
             at = slice(8 * b, 8 * b + 8)

time: 65.1 us -> 64.5 us (level)
  no operation moved by 1% of the time
where the time goes in v5:
time: 64.5 us; the launch traced here: 64.8 us
  Pallas kernels  64.1 us (99%)
  between operations  0.66 us (1%)
    pallas_call x4, Pallas kernels, call(): pl.pallas_call(kernel, out_shape=outs, in_specs=in_specs or [VMEM] * len(...  64.1 us

profile of v5, /device:TPU:1, one launch (start us, length us, event | category | flops | bytes accessed | tf_op | source)
XLA Modules:
  0.0 64.8 jit_solution(743438204580846770)
XLA Ops:
  0.6 22.9 %first_kernel.1 = (f32[128,2,128]{2,1,0:T(2,128)}, f32[32,256]{1,0:T(8,128)}, f32[288,256]{1,0:T(8,128)}, f32[288,256]{1,0:T(8,128)}, f32[3,32,16,128]{3,2,1,0:T...) custom-call(f32[3,32,16,128]{3,2,1,0:T(8,128)} %grad_cells.3, f32[3,1024]{1,0:T(4,128)} %grad_segs.3, ...), custom_call_target="tpu_custom_call" | custom-call | tf_op jit(solution)/shard_map/first_kernel/pallas_call | solution.py:887
  23.6 9.4 %second_kernel.1 = (f32[3,32,16,128]{3,2,1,0:T(8,128)}, f32[240,256]{1,0:T(8,128)}, f32[40,256]{1,0:T(8,128)}, s32[32,256]{1,0:T(8,128)}, s32[8]{0:T(128)}) custom-call(f32[128,2,128]{2,1,0:T(2,128)} %get-tuple-element.23.came, f32[3,3,32,16,128]{4,3,2,1,0:T(8,128)} %diag.5, f32[3,32,16,128]{3,2,1,0:T(8,128)} %get-tuple-element.24.adjoint, ...), custom_call_target="tpu_custom_call" | custom-call | tf_op jit(solution)/shard_map/second_kernel/pallas_call | solution.py:887
  32.9 28.2 %third_kernel.1 = (f32[120,256]{1,0:T(8,128)}, f32[3,32,16,128]{3,2,1,0:T(8,128)}, f32[3,1024]{1,0:T(4,128)}, f32[3,1024]{1,0:T(4,128)}) custom-call(f32[240,256]{1,0:T(8,128)} %get-tuple-element.28.pulled, s32[32,256]{1,0:T(8,128)} %get-tuple-element.29.place, f32[3,32,16,128]{3,2,1,0:T(8,128)} %grad_cells.3, f32[3,32,16,128]{3,2,1,0:T(8,128)} %get-tuple-element.19.adjoint, ...), custom_call_target="tpu_custom_call" | custom-call | tf_op jit(solution)/shard_map/third_kernel/pallas_call | solution.py:887
  61.1 3.6 %fourth_kernel.1 = (f32[3,32,16,128]{3,2,1,0:T(8,128)}, f32[3,1024]{1,0:T(4,128)}, f32[3,1024]{1,0:T(4,128)}) custom-call(s32[8]{0:T(128)} %get-tuple-element.27.starts, f32[120,256]{1,0:T(8,128)} %get-tuple-element.34.ordered, f32[3,32,16,128]{3,2,1,0:T(8,128)} %get-tuple-element.35.rest, f32[40,256]{1,0:T(8,128)} %get-tuple-element.36.index_rows, ...), custom_call_target="tpu_custom_call" | custom-call | tf_op jit(solution)/shard_map/fourth_kernel/pallas_call | solution.py:887
